TPU v7x, 32 devices: a whole 2x2x4 slice. The times are simulated.
32 devices in a mesh: dp: 8 (over z, x), tensor: 4 (over y, core).
Axes of the slice: x: 2, y: 2, z: 4, core: 2. Of those that a mesh axis runs over, the one named last changes fastest.
Arguments:
- frames_input: bfloat16 [8192, 1024], P(('dp', 'tensor')), may hold values from -6 to 6
- out_grad: bfloat16 [8192, 1024], P(('dp', 'tensor')), may hold values from -6 to 6
- lengths: int32 [8], P('dp'), may hold values from 341 to 1024, as said below
- step_count: int32 [1], replicated, may hold values from 2 to 4
- rates: float32 [4], replicated, may hold values from 0.4 to 0.6
- expand_params: float32 [2, 2, 1024, 4096], P(None, None, 'dp', 'tensor'), may hold values from -0.1875 to 0.1875
- expand_first: float32 [2, 1024, 4096], P(None, 'dp', 'tensor'), may hold values from -80 to 80
- expand_second: float32 [2, 1024, 4096], P(None, 'dp', 'tensor'), may hold values from 81.92 to 1310.72
- shrink_params: float32 [2, 2, 4096, 1024], P(None, None, 'tensor', 'dp'), may hold values from -0.1875 to 0.1875
- shrink_first: float32 [2, 4096, 1024], P(None, 'tensor', 'dp'), may hold values from -80 to 80
- shrink_second: float32 [2, 4096, 1024], P(None, 'tensor', 'dp'), may hold values from 81.92 to 1310.72
- project_params: float32 [2, 3, 1024, 1024], P(None, None, 'dp', 'tensor'), may hold values from -0.1875 to 0.1875
- project_first: float32 [3, 1024, 1024], P(None, 'dp', 'tensor'), may hold values from -32 to 32
- project_second: float32 [3, 1024, 1024], P(None, 'dp', 'tensor'), may hold values from 12.288 to 196.608
- mixing_params: float32 [2, 1024, 1024], P(None, 'tensor', 'dp'), may hold values from -0.5 to 0.5
- mixing_first: float32 [1024, 1024], P('tensor', 'dp'), may hold values from -56 to 56
- mixing_second: float32 [1024, 1024], P('tensor', 'dp'), may hold values from 40.96 to 655.36
- gating_params: float32 [2, 2, 1024, 1024], P(None, None, 'dp', 'tensor'), may hold values from -0.1875 to 0.1875
- gating_first: float32 [2, 1024, 1024], P(None, 'dp', 'tensor'), may hold values from -56 to 56
- gating_second: float32 [2, 1024, 1024], P(None, 'dp', 'tensor'), may hold values from 40.96 to 655.36
- kernel_params: float32 [2, 31, 1024], P(None, None, 'tensor'), may hold values from -1 to 1
- kernel_first: float32 [31, 1024], P(None, 'tensor'), may hold values from -56 to 56
- kernel_second: float32 [31, 1024], P(None, 'tensor'), may hold values from 40.96 to 655.36
- merging_params: float32 [2, 1024, 1024], P(None, 'tensor', 'dp'), may hold values from -0.375 to 0.375
- merging_first: float32 [1024, 1024], P('tensor', 'dp'), may hold values from -56 to 56
- merging_second: float32 [1024, 1024], P('tensor', 'dp'), may hold values from 40.96 to 655.36
- gains_params: float32 [2, 5, 1024], replicated, may hold values from 0.5 to 1.5
- gains_first: float32 [5, 1024], replicated, may hold values from -256 to 256
- gains_second: float32 [5, 1024], replicated, may hold values from 819.2 to 13107.2
Outputs:
- frames_out: bfloat16 [8192, 1024], P(('dp', 'tensor'))
- input_grad: bfloat16 [8192, 1024], P(('dp', 'tensor'))
- expand_grad: float32 [2, 1024, 4096], P(None, 'dp', 'tensor')
- expand_mean: float32 [2, 1024, 4096], P(None, 'dp', 'tensor')
- expand_square: float32 [2, 1024, 4096], P(None, 'dp', 'tensor')
- expand_weights: float32 [2, 2, 1024, 4096], P(None, None, 'dp', 'tensor')
- expand_copies: bfloat16 [2, 2, 1024, 4096], P(None, None, 'dp', 'tensor')
- shrink_grad: float32 [2, 4096, 1024], P(None, 'tensor', 'dp')
- shrink_mean: float32 [2, 4096, 1024], P(None, 'tensor', 'dp')
- shrink_square: float32 [2, 4096, 1024], P(None, 'tensor', 'dp')
- shrink_weights: float32 [2, 2, 4096, 1024], P(None, None, 'tensor', 'dp')
- shrink_copies: bfloat16 [2, 2, 4096, 1024], P(None, None, 'tensor', 'dp')
- project_grad: float32 [3, 1024, 1024], P(None, 'dp', 'tensor')
- project_mean: float32 [3, 1024, 1024], P(None, 'dp', 'tensor')
- project_square: float32 [3, 1024, 1024], P(None, 'dp', 'tensor')
- project_weights: float32 [2, 3, 1024, 1024], P(None, None, 'dp', 'tensor')
- project_copies: bfloat16 [2, 3, 1024, 1024], P(None, None, 'dp', 'tensor')
- mixing_grad: float32 [1024, 1024], P('tensor', 'dp')
- mixing_mean: float32 [1024, 1024], P('tensor', 'dp')
- mixing_square: float32 [1024, 1024], P('tensor', 'dp')
- mixing_weights: float32 [2, 1024, 1024], P(None, 'tensor', 'dp')
- mixing_copies: bfloat16 [2, 1024, 1024], P(None, 'tensor', 'dp')
- gating_grad: float32 [2, 1024, 1024], P(None, 'dp', 'tensor')
- gating_mean: float32 [2, 1024, 1024], P(None, 'dp', 'tensor')
- gating_square: float32 [2, 1024, 1024], P(None, 'dp', 'tensor')
- gating_weights: float32 [2, 2, 1024, 1024], P(None, None, 'dp', 'tensor')
- gating_copies: bfloat16 [2, 2, 1024, 1024], P(None, None, 'dp', 'tensor')
- kernel_grad: float32 [31, 1024], P(None, 'tensor')
- kernel_mean: float32 [31, 1024], P(None, 'tensor')
- kernel_square: float32 [31, 1024], P(None, 'tensor')
- kernel_weights: float32 [2, 31, 1024], P(None, None, 'tensor')
- kernel_copies: bfloat16 [2, 31, 1024], P(None, None, 'tensor')
- merging_grad: float32 [1024, 1024], P('tensor', 'dp')
- merging_mean: float32 [1024, 1024], P('tensor', 'dp')
- merging_square: float32 [1024, 1024], P('tensor', 'dp')
- merging_weights: float32 [2, 1024, 1024], P(None, 'tensor', 'dp')
- merging_copies: bfloat16 [2, 1024, 1024], P(None, 'tensor', 'dp')
- gains_grad: float32 [5, 1024], replicated
- gains_mean: float32 [5, 1024], replicated
- gains_square: float32 [5, 1024], replicated
- gains_weights: float32 [2, 5, 1024], replicated
- gains_copies: bfloat16 [2, 5, 1024], replicated
- trust_norms: float32 [17, 2], replicated
Inputs may be any that keep to these rules, and one draw needn't show every extreme that they name: `lengths`: each item's length lies between 341 and 1024; some item fills its whole slot.
All inputs are finite; a program needn't handle non-finite values.
Results may differ from a plain program's by a relative error of at most 0.014.
Values may be sent and summed in bfloat16 or wider, within the bound.
A program may use at most 192 MiB of HBM per device.

v0:
```python
import jax
import jax.numpy as jnp
from jax import lax
from jax.sharding import PartitionSpec as P

HEAD_DIM = 64
KERNEL = 31
SLOT = 1024
ITEMS_DEV = 1
BLOCK = 512


EPSILON = 1e-05
ADAM_EPS = 1e-06
DECAY_RATE = 0.01
MASKED = -1000000000.0


def product(operand, another):
    return jnp.dot(operand, another, preferred_element_type=jnp.float32)


def product_left(operand, another):
    return lax.dot_general(
        operand, another, (((0,), (0,)), ((), ())), preferred_element_type=jnp.float32
    )


def product_right(operand, another):
    return lax.dot_general(
        operand, another, (((1,), (1,)), ((), ())), preferred_element_type=jnp.float32
    )


def silu_slope(before):
    sigmoid_of = jax.nn.sigmoid(before)
    return sigmoid_of * (1.0 + before * (1.0 - sigmoid_of))


def normalize(hidden, gain_row):
    center = hidden - jnp.mean(hidden, axis=-1, keepdims=True)
    spread = jnp.mean(center * center, axis=-1, keepdims=True)
    inverse = lax.rsqrt(spread + EPSILON)
    unit_rows = center * inverse
    return (unit_rows * gain_row, unit_rows, inverse)


def normalize_back(upstream, unit_rows, inverse, gain_row):
    gain_grad = jnp.sum(upstream * unit_rows, axis=0)
    scaled = upstream * gain_row
    centered = (
        scaled
        - jnp.mean(scaled, axis=-1, keepdims=True)
        - unit_rows * jnp.mean(scaled * unit_rows, axis=-1, keepdims=True)
    )
    return (centered * inverse, gain_grad)


def enter_rows(normed):
    result = lax.all_gather(normed.astype(jnp.bfloat16), "tensor", axis=0, tiled=True)
    return result


def leave_rows(partial_sum):
    result = lax.psum_scatter(partial_sum, "tensor", scatter_dimension=0, tiled=True)
    return result


def enter_grads(upstream):
    result = lax.all_gather(upstream.astype(jnp.bfloat16), "tensor", axis=0, tiled=True)
    return result


def leave_grads(partial_sum):
    result = lax.psum_scatter(partial_sum, "tensor", scatter_dimension=0, tiled=True)
    return result


def feed_forward(gathered, expand_matrix, shrink_matrix):
    before = product(gathered, expand_matrix)
    hidden = jax.nn.silu(before).astype(jnp.bfloat16)
    return (product(hidden, shrink_matrix), (before, hidden))


def feed_back(gathered, expand_matrix, shrink_matrix, kept_rows, upstream):
    before, hidden = kept_rows
    shrink_grad = product_left(hidden, upstream)
    before_grad = (product_right(upstream, shrink_matrix) * silu_slope(before)).astype(jnp.bfloat16)
    expand_grad = product_left(gathered, before_grad)
    return (product_right(before_grad, expand_matrix), expand_grad, shrink_grad)


def attend_item(queries, keys_all, values_all, live_keys):
    score_scale = HEAD_DIM ** (-0.5)
    heads_local = queries.shape[1]
    blocks = queries.reshape(SLOT // BLOCK, BLOCK, heads_local, HEAD_DIM)

    def one_block(query_block):
        scores = (
            jnp.einsum("bhe,khe->hbk", query_block, keys_all, preferred_element_type=jnp.float32)
            * score_scale
        )
        scores = jnp.where(live_keys[None, None, :], scores, MASKED)
        row_peak = jnp.max(scores, axis=-1, keepdims=True)
        exponent = jnp.exp(scores - row_peak)
        row_total = jnp.sum(exponent, axis=-1, keepdims=True)
        weights = (exponent / row_total).astype(jnp.bfloat16)
        output = jnp.einsum("hbk,khe->bhe", weights, values_all, preferred_element_type=jnp.float32)
        return (output, (row_peak + jnp.log(row_total))[..., 0])

    outputs, logsum = lax.map(one_block, blocks)
    return (outputs.reshape(SLOT, heads_local, HEAD_DIM), logsum)


def attend_back(queries, keys_all, values_all, live_keys, logsum, grad_out, count):
    score_scale = HEAD_DIM ** (-0.5)
    heads_local = queries.shape[1]
    blocks = queries.reshape(SLOT // BLOCK, BLOCK, heads_local, HEAD_DIM)
    grad_blocks = grad_out.reshape(SLOT // BLOCK, BLOCK, heads_local, HEAD_DIM)

    def one_block(carried, inputs):
        key_grad, value_grad = carried
        query_block, grad_block, logsum_block = inputs
        scores = (
            jnp.einsum("bhe,khe->hbk", query_block, keys_all, preferred_element_type=jnp.float32)
            * score_scale
        )
        scores = jnp.where(live_keys[None, None, :], scores, MASKED)
        probability = jnp.exp(scores - logsum_block[..., None])
        weights = probability.astype(jnp.bfloat16)
        value_grad = value_grad + jnp.einsum(
            "hbk,bhe->khe", weights, grad_block, preferred_element_type=jnp.float32
        )
        prob_grad = jnp.einsum(
            "bhe,khe->hbk", grad_block, values_all, preferred_element_type=jnp.float32
        )
        row_inner = jnp.sum(probability * prob_grad, axis=-1, keepdims=True)
        score_grad = (probability * (prob_grad - row_inner)).astype(jnp.bfloat16)
        query_grad = (
            jnp.einsum("hbk,khe->bhe", score_grad, keys_all, preferred_element_type=jnp.float32)
            * score_scale
        )
        key_grad = (
            key_grad
            + jnp.einsum(
                "hbk,bhe->khe", score_grad, query_block, preferred_element_type=jnp.float32
            )
            * score_scale
        )
        return ((key_grad, value_grad), query_grad)

    zeroed = jnp.zeros((count, heads_local, HEAD_DIM), jnp.float32)
    (key_grad, value_grad), query_grad = lax.scan(
        one_block, (zeroed, zeroed), (blocks, grad_blocks, logsum)
    )
    return (query_grad.reshape(SLOT, heads_local, HEAD_DIM), key_grad, value_grad)


def attend_pick(queries, keys_all, values_all, live_keys):
    result = attend_item(queries, keys_all, values_all, live_keys)
    return result


def back_pick(queries, keys_all, values_all, live_keys, logsum, grad_out):
    result = attend_back(queries, keys_all, values_all, live_keys, logsum, grad_out, SLOT)
    return result


def attention_forward(gathered, project_matrix, mixing_matrix, live_keys):
    packed = jnp.einsum(
        "gd,kde->kge", gathered, project_matrix, preferred_element_type=jnp.float32
    ).astype(jnp.bfloat16)
    heads_local = packed.shape[2] // HEAD_DIM
    shaped = packed.reshape(3, ITEMS_DEV, SLOT, heads_local, HEAD_DIM)
    output, logsum = attend_pick(shaped[0, 0], shaped[1, 0], shaped[2, 0], live_keys[0])
    outputs = [output]
    logsums = [logsum]
    mixed_heads = jnp.stack(outputs).reshape(packed.shape[1], packed.shape[2]).astype(jnp.bfloat16)
    return (product(mixed_heads, mixing_matrix), (packed, mixed_heads, logsums))


def attention_back(gathered, project_matrix, mixing_matrix, live_keys, kept_rows, upstream):
    packed, mixed_heads, logsums = kept_rows
    mixing_grad = product_left(mixed_heads, upstream)
    mixed_grad = product_right(upstream, mixing_matrix).astype(jnp.bfloat16)
    heads_local = packed.shape[2] // HEAD_DIM
    shaped = packed.reshape(3, ITEMS_DEV, SLOT, heads_local, HEAD_DIM)
    grad_shaped = mixed_grad.reshape(ITEMS_DEV, SLOT, heads_local, HEAD_DIM)
    query_grad, key_grad, value_grad = back_pick(
        shaped[0, 0], shaped[1, 0], shaped[2, 0], live_keys[0], logsums[0], grad_shaped[0]
    )
    pieces = [jnp.stack([query_grad, key_grad, value_grad])]
    packed_grad = jnp.stack(pieces, axis=1).reshape(packed.shape).astype(jnp.bfloat16)
    project_grad = jnp.einsum(
        "gd,kge->kde", gathered, packed_grad, preferred_element_type=jnp.float32
    )
    gathered_grad = jnp.einsum(
        "kge,kde->gd", packed_grad, project_matrix, preferred_element_type=jnp.float32
    )
    return (gathered_grad, project_grad, mixing_grad)


def conv_forward(gathered, gating_matrix, kernel_taps, merging_matrix, live_group):
    gated_pair = jnp.einsum(
        "gd,kdc->kgc", gathered, gating_matrix, preferred_element_type=jnp.float32
    )
    sigmoid_gate = jax.nn.sigmoid(gated_pair[1])
    glu_values = gated_pair[0] * sigmoid_gate * live_group
    channels = glu_values.shape[1]
    margin = (KERNEL - 1) // 2
    padded = jnp.pad(
        glu_values.reshape(ITEMS_DEV, SLOT, channels), ((0, 0), (margin, margin), (0, 0))
    )
    mixed_time = padded[:, 0:SLOT] * kernel_taps[0]
    for offset in range(1, KERNEL):
        mixed_time = mixed_time + padded[:, offset : offset + SLOT] * kernel_taps[offset]
    mixed_time = mixed_time.reshape(-1, channels)
    hidden = jax.nn.silu(mixed_time).astype(jnp.bfloat16)
    return (product(hidden, merging_matrix), (gated_pair, sigmoid_gate, padded, mixed_time, hidden))


def conv_back(
    gathered, gating_matrix, kernel_taps, merging_matrix, live_group, kept_rows, upstream
):
    gated_pair, sigmoid_gate, padded, mixed_time, hidden = kept_rows
    merging_grad = product_left(hidden, upstream)
    time_grad = product_right(upstream, merging_matrix) * silu_slope(mixed_time)
    channels = time_grad.shape[1]
    margin = (KERNEL - 1) // 2
    slope_items = time_grad.reshape(ITEMS_DEV, SLOT, channels)
    kernel_grad = jnp.stack(
        [
            jnp.sum(padded[:, offset : offset + SLOT] * slope_items, axis=(0, 1))
            for offset in range(KERNEL)
        ]
    )
    slope_padded = jnp.pad(slope_items, ((0, 0), (margin, margin), (0, 0)))
    glu_grad = slope_padded[:, 2 * margin : 2 * margin + SLOT] * kernel_taps[0]
    for offset in range(1, KERNEL):
        glu_grad = (
            glu_grad
            + slope_padded[:, 2 * margin - offset : 2 * margin - offset + SLOT]
            * kernel_taps[offset]
        )
    glu_grad = glu_grad.reshape(-1, channels) * live_group
    gated_grad = jnp.stack(
        [glu_grad * sigmoid_gate, glu_grad * gated_pair[0] * sigmoid_gate * (1.0 - sigmoid_gate)]
    ).astype(jnp.bfloat16)
    gating_grad = jnp.einsum(
        "gd,kgc->kdc", gathered, gated_grad, preferred_element_type=jnp.float32
    )
    gathered_grad = jnp.einsum(
        "kgc,kdc->gd", gated_grad, gating_matrix, preferred_element_type=jnp.float32
    )
    return (gathered_grad, gating_grad, kernel_grad, merging_grad)


def piece_squares(numbers, stacked):
    pieces_count = numbers.shape[0] if stacked else 1
    return jnp.sum(jnp.reshape(numbers * numbers, (pieces_count, -1)), axis=1)


def shards(
    frames_input,
    out_grad,
    lengths,
    step_count,
    rates,
    expand_params,
    expand_first,
    expand_second,
    shrink_params,
    shrink_first,
    shrink_second,
    project_params,
    project_first,
    project_second,
    mixing_params,
    mixing_first,
    mixing_second,
    gating_params,
    gating_first,
    gating_second,
    kernel_params,
    kernel_first,
    kernel_second,
    merging_params,
    merging_first,
    merging_second,
    gains_params,
    gains_first,
    gains_second,
):
    local_rows = frames_input.shape[0]
    tensor_rank = lax.axis_index("tensor")
    data_rank = lax.axis_index("dp")
    positions = jnp.arange(SLOT, dtype=jnp.int32)
    live_keys = positions[None, :] < lengths[:, None]
    live_group = live_keys.astype(jnp.float32).reshape(-1, 1)
    live_local = lax.dynamic_slice_in_dim(live_group, tensor_rank * local_rows, local_rows, 0)
    expand_matrix, shrink_matrix, project_matrix, mixing_matrix, gating_matrix, merging_matrix = (
        lax.all_gather(expand_params[0].astype(jnp.bfloat16), "dp", axis=1, tiled=True),
        lax.all_gather(shrink_params[0].astype(jnp.bfloat16), "dp", axis=2, tiled=True),
        lax.all_gather(project_params[0].astype(jnp.bfloat16), "dp", axis=1, tiled=True),
        lax.all_gather(mixing_params[0].astype(jnp.bfloat16), "dp", axis=1, tiled=True),
        lax.all_gather(gating_params[0].astype(jnp.bfloat16), "dp", axis=1, tiled=True),
        lax.all_gather(merging_params[0].astype(jnp.bfloat16), "dp", axis=1, tiled=True),
    )
    kernel_taps = kernel_params[0]
    gain_rows = gains_params[0]
    initial = frames_input.astype(jnp.float32)
    cotangent = out_grad.astype(jnp.float32)
    normed, unit_one, inverse_one = normalize(initial, gain_rows[0])
    rows_one = enter_rows(normed)
    branch_out, kept_one = feed_forward(rows_one, expand_matrix[0], shrink_matrix[0])
    after_one = initial + 0.5 * leave_rows(branch_out)
    normed, unit_two, inverse_two = normalize(after_one, gain_rows[1])
    rows_two = enter_rows(normed)
    branch_out, kept_two = attention_forward(rows_two, project_matrix, mixing_matrix, live_keys)
    after_two = after_one + leave_rows(branch_out)
    normed, unit_three, inverse_three = normalize(after_two, gain_rows[2])
    rows_three = enter_rows(normed)
    branch_out, kept_three = conv_forward(
        rows_three, gating_matrix, kernel_taps, merging_matrix, live_group
    )
    after_three = after_two + leave_rows(branch_out)
    normed, unit_four, inverse_four = normalize(after_three, gain_rows[3])
    rows_four = enter_rows(normed)
    branch_out, kept_four = feed_forward(rows_four, expand_matrix[1], shrink_matrix[1])
    after_four = after_three + 0.5 * leave_rows(branch_out)
    normed_out, unit_five, inverse_five = normalize(after_four, gain_rows[4])
    upstream = cotangent * live_local
    residual, gain_five = normalize_back(upstream, unit_five, inverse_five, gain_rows[4])
    rows_grad, expand_two, shrink_two = feed_back(
        rows_four, expand_matrix[1], shrink_matrix[1], kept_four, enter_grads(0.5 * residual)
    )
    normed_grad, gain_four = normalize_back(
        leave_grads(rows_grad), unit_four, inverse_four, gain_rows[3]
    )
    residual = residual + normed_grad
    rows_grad, gating_grad, kernel_grad, merging_grad = conv_back(
        rows_three,
        gating_matrix,
        kernel_taps,
        merging_matrix,
        live_group,
        kept_three,
        enter_grads(residual),
    )
    normed_grad, gain_three = normalize_back(
        leave_grads(rows_grad), unit_three, inverse_three, gain_rows[2]
    )
    residual = residual + normed_grad
    rows_grad, project_grad, mixing_grad = attention_back(
        rows_two, project_matrix, mixing_matrix, live_keys, kept_two, enter_grads(residual)
    )
    normed_grad, gain_two = normalize_back(
        leave_grads(rows_grad), unit_two, inverse_two, gain_rows[1]
    )
    residual = residual + normed_grad
    rows_grad, expand_one, shrink_one = feed_back(
        rows_one, expand_matrix[0], shrink_matrix[0], kept_one, enter_grads(0.5 * residual)
    )
    normed_grad, gain_one = normalize_back(
        leave_grads(rows_grad), unit_one, inverse_one, gain_rows[0]
    )
    residual = residual + normed_grad
    frames_out = normed_out.astype(jnp.bfloat16)
    input_grad = residual.astype(jnp.bfloat16)
    expand_grad = jnp.stack([expand_one, expand_two])
    shrink_grad = jnp.stack([shrink_one, shrink_two])
    expand_sum, shrink_sum, project_sum, mixing_sum, gating_sum, merging_sum = (
        lax.psum_scatter(expand_grad, "dp", scatter_dimension=1, tiled=True),
        lax.psum_scatter(shrink_grad, "dp", scatter_dimension=2, tiled=True),
        lax.psum_scatter(project_grad, "dp", scatter_dimension=1, tiled=True),
        lax.psum_scatter(mixing_grad, "dp", scatter_dimension=1, tiled=True),
        lax.psum_scatter(gating_grad, "dp", scatter_dimension=1, tiled=True),
        lax.psum_scatter(merging_grad, "dp", scatter_dimension=1, tiled=True),
    )
    gains_grad = jnp.stack([gain_one, gain_two, gain_three, gain_four, gain_five])
    gains_sum, kernel_sum = lax.psum((gains_grad, kernel_grad), "dp")
    gains_sum = lax.psum(gains_sum, "tensor")
    beta_one = rates[0]
    beta_two = rates[1]
    average_rate = rates[2]
    learn_rate = rates[3]
    steps_done = step_count[0].astype(jnp.float32)
    bias_one = 1.0 - beta_one**steps_done
    bias_two = 1.0 - beta_two**steps_done
    first_data = (data_rank == 0).astype(jnp.float32)
    first_device = first_data * (tensor_rank == 0).astype(jnp.float32)
    entries = [
        (expand_sum, expand_params, expand_first, expand_second, True, DECAY_RATE, 1.0),
        (shrink_sum, shrink_params, shrink_first, shrink_second, True, DECAY_RATE, 1.0),
        (project_sum, project_params, project_first, project_second, True, DECAY_RATE, 1.0),
        (mixing_sum, mixing_params, mixing_first, mixing_second, False, DECAY_RATE, 1.0),
        (gating_sum, gating_params, gating_first, gating_second, True, DECAY_RATE, 1.0),
        (kernel_sum, kernel_params, kernel_first, kernel_second, False, DECAY_RATE, first_data),
        (merging_sum, merging_params, merging_first, merging_second, False, DECAY_RATE, 1.0),
        (gains_sum, gains_params, gains_first, gains_second, True, 0.0, first_device),
    ]
    moments = []
    weight_parts = []
    update_parts = []
    for gradient, params, first, second, stacked, decay_weight, owner_mask in entries:
        mean_new = beta_one * first + (1.0 - beta_one) * gradient
        square_new = beta_two * second + (1.0 - beta_two) * gradient * gradient
        direction = (
            mean_new / bias_one / (jnp.sqrt(square_new / bias_two) + ADAM_EPS)
            + decay_weight * params[0]
        )
        moments.append((mean_new, square_new, direction))
        weight_parts.append(piece_squares(params[0], stacked) * owner_mask)
        update_parts.append(piece_squares(direction, stacked) * owner_mask)
    weight_total, update_total = lax.psum(
        (jnp.concatenate(weight_parts), jnp.concatenate(update_parts)), ("dp", "tensor")
    )
    weight_norm = jnp.sqrt(weight_total)
    update_norm = jnp.sqrt(update_total)
    trust_all = weight_norm / update_norm
    results = []
    offset_now = 0
    for position in range(len(entries)):
        gradient, params, first, second, stacked, decay_weight, owner_mask = entries[position]
        mean_new, square_new, direction = moments[position]
        master = params[0]
        if stacked:
            pieces_count = master.shape[0]
            broadcast_shape = (pieces_count,) + (1,) * (master.ndim - 1)
        else:
            pieces_count = 1
            broadcast_shape = (1,) * master.ndim
        trust_ratio = trust_all[offset_now : offset_now + pieces_count].reshape(broadcast_shape)
        offset_now = offset_now + pieces_count
        master_new = master - learn_rate * trust_ratio * direction
        average_new = average_rate * params[1] + (1.0 - average_rate) * master_new
        weights_new = jnp.stack([master_new, average_new])
        results.extend(
            [gradient, mean_new, square_new, weights_new, weights_new.astype(jnp.bfloat16)]
        )
    trust_norms = jnp.stack([weight_norm, update_norm], axis=1)
    return (
        frames_out,
        input_grad,
        results[0],
        results[1],
        results[2],
        results[3],
        results[4],
        results[5],
        results[6],
        results[7],
        results[8],
        results[9],
        results[10],
        results[11],
        results[12],
        results[13],
        results[14],
        results[15],
        results[16],
        results[17],
        results[18],
        results[19],
        results[20],
        results[21],
        results[22],
        results[23],
        results[24],
        results[25],
        results[26],
        results[27],
        results[28],
        results[29],
        results[30],
        results[31],
        results[32],
        results[33],
        results[34],
        results[35],
        results[36],
        results[37],
        results[38],
        results[39],
        trust_norms,
    )


def solution(mesh):
    return jax.shard_map(
        shards,
        mesh=mesh,
        in_specs=(
            P(("dp", "tensor"), None),
            P(("dp", "tensor"), None),
            P("dp"),
            P(),
            P(),
            P(None, None, "dp", "tensor"),
            P(None, "dp", "tensor"),
            P(None, "dp", "tensor"),
            P(None, None, "tensor", "dp"),
            P(None, "tensor", "dp"),
            P(None, "tensor", "dp"),
            P(None, None, "dp", "tensor"),
            P(None, "dp", "tensor"),
            P(None, "dp", "tensor"),
            P(None, "tensor", "dp"),
            P("tensor", "dp"),
            P("tensor", "dp"),
            P(None, None, "dp", "tensor"),
            P(None, "dp", "tensor"),
            P(None, "dp", "tensor"),
            P(None, None, "tensor"),
            P(None, "tensor"),
            P(None, "tensor"),
            P(None, "tensor", "dp"),
            P("tensor", "dp"),
            P("tensor", "dp"),
            P(),
            P(),
            P(),
        ),
        out_specs=(
            P(("dp", "tensor"), None),
            P(("dp", "tensor"), None),
            P(None, "dp", "tensor"),
            P(None, "dp", "tensor"),
            P(None, "dp", "tensor"),
            P(None, None, "dp", "tensor"),
            P(None, None, "dp", "tensor"),
            P(None, "tensor", "dp"),
            P(None, "tensor", "dp"),
            P(None, "tensor", "dp"),
            P(None, None, "tensor", "dp"),
            P(None, None, "tensor", "dp"),
            P(None, "dp", "tensor"),
            P(None, "dp", "tensor"),
            P(None, "dp", "tensor"),
            P(None, None, "dp", "tensor"),
            P(None, None, "dp", "tensor"),
            P("tensor", "dp"),
            P("tensor", "dp"),
            P("tensor", "dp"),
            P(None, "tensor", "dp"),
            P(None, "tensor", "dp"),
            P(None, "dp", "tensor"),
            P(None, "dp", "tensor"),
            P(None, "dp", "tensor"),
            P(None, None, "dp", "tensor"),
            P(None, None, "dp", "tensor"),
            P(None, "tensor"),
            P(None, "tensor"),
            P(None, "tensor"),
            P(None, None, "tensor"),
            P(None, None, "tensor"),
            P("tensor", "dp"),
            P("tensor", "dp"),
            P("tensor", "dp"),
            P(None, "tensor", "dp"),
            P(None, "tensor", "dp"),
            P(),
            P(),
            P(),
            P(),
            P(),
            P(),
        ),
        check_vma=False,
    )
```

profile of v0, /device:TPU:0, one launch (start us, length us, event | category | flops | bytes accessed | tf_op | source)
XLA Modules:
  0.0 1636.4 jit_solution(9339554696162872349)
XLA Ops:
  17.7 21.1 %all-gather.13.cloned.1.call-done = bf16[1024,1024]{1,0:T(8,128)(2,1)} async-done(((bf16[256,1024]{1,0:T(8,128)(2,1)}), bf16[1024,1024]{1,0:T(8,128)(2,1)}) %all-gather.13.cloned.1.call-update) | async-done | bytes 2097168 | tf_op jit(solution)/shard_map/all_gather | solution.py:60
  38.8 76.2 %all-gather.15.cloned.1.call-done = bf16[2,1024,1024]{2,1,0:T(8,128)(2,1)} async-done(((bf16[2,128,1024]{2,1,0:T(8,128)(2,1)}), bf16[2,1024,1024]{2,1,0:T(8,128)(2,1)}) %all-gather.15.cloned.1.call-update) | async-done | bytes 4194320 | tf_op jit(solution)/shard_map/all_gather | solution.py:302
  121.5 69.5 %all-gather.17.cloned.1.call-done = bf16[2,1024,1024]{2,1,0:T(8,128)(2,1)} async-done(((bf16[2,1024,128]{2,1,0:T(8,128)(2,1)}), bf16[2,1024,1024]{2,1,0:T(8,128)(2,1)}) %all-gather.17.cloned.1.call-update) | async-done | bytes 4194320 | tf_op jit(solution)/shard_map/all_gather | solution.py:303
  201.6 39.3 %reduce-scatter.15.cloned.1.call-done = f32[256,1024]{1,0:T(8,128)} async-done(((f32[1024,1024]{1,0:T(8,128)}), f32[256,1024]{1,0:T(8,128)}) %reduce-scatter.15.cloned.1.call-update) | async-done | bytes 1048592 | tf_op jit(solution)/shard_map/reduce_scatter | solution.py:65
  244.7 30.0 %all_gather.47 = bf16[256,1024]{1,0:T(8,128)(2,1)} all-gather(bf16[256,128]{1,0:T(8,128)(2,1)S(1)} %bitcast_convert_fusion.5), channel_id=1, replica_groups=mesh['dp'=8,'tensor'=4] {'dp'}, dimensions={1}, use_global_device_ids=true | all-gather | bytes 589824 | tf_op jit(solution)/shard_map/all_gather | solution.py:305
  274.7 17.3 %all-gather.21.cloned.1.call-done = bf16[3,1024,256]{1,2,0:T(8,128)(2,1)} async-done(((bf16[3,128,256]{1,2,0:T(8,128)(2,1)}), bf16[3,1024,256]{1,2,0:T(8,128)(2,1)}) %all-gather.21.cloned.1.call-update) | async-done | bytes 1572880 | tf_op jit(solution)/shard_map/all_gather | solution.py:304
  292.0 22.9 %all-gather.19.cloned.1.call-done = bf16[1024,1024]{1,0:T(8,128)(2,1)} async-done(((bf16[256,1024]{1,0:T(8,128)(2,1)}), bf16[1024,1024]{1,0:T(8,128)(2,1)}) %all-gather.19.cloned.1.call-update) | async-done | bytes 2097168 | tf_op jit(solution)/shard_map/all_gather | solution.py:60
  321.3 13.3 while.28
  340.9 42.9 %reduce-scatter.17.cloned.1.call-done = f32[256,1024]{1,0:T(8,128)} async-done(((f32[1024,1024]{1,0:T(8,128)}), f32[256,1024]{1,0:T(8,128)}) %reduce-scatter.17.cloned.1.call-update) | async-done | bytes 1048592 | tf_op jit(solution)/shard_map/reduce_scatter | solution.py:65
  388.2 29.5 %all_gather.50 = bf16[256,1024]{1,0:T(8,128)(2,1)S(1)} all-gather(bf16[256,128]{1,0:T(8,128)(2,1)S(1)} %bitcast_convert_fusion.4), channel_id=1, replica_groups=mesh['dp'=8,'tensor'=4] {'dp'}, dimensions={1}, use_global_device_ids=true | all-gather | bytes 589824 | tf_op jit(solution)/shard_map/all_gather | solution.py:307
  417.7 11.4 all-gather.25.cloned.1.call-done
  429.1 23.5 %all-gather.23.cloned.1.call-done = bf16[1024,1024]{1,0:T(8,128)(2,1)} async-done(((bf16[256,1024]{1,0:T(8,128)(2,1)}), bf16[1024,1024]{1,0:T(8,128)(2,1)}) %all-gather.23.cloned.1.call-update) | async-done | bytes 2097168 | tf_op jit(solution)/shard_map/all_gather | solution.py:60
  466.1 44.6 %reduce-scatter.19.cloned.1.call-done = f32[256,1024]{1,0:T(8,128)} async-done(((f32[1024,1024]{1,0:T(8,128)}), f32[256,1024]{1,0:T(8,128)}) %reduce-scatter.19.cloned.1.call-update) | async-done | bytes 1048592 | tf_op jit(solution)/shard_map/reduce_scatter | solution.py:65
  513.5 22.7 %all-gather.27.cloned.1.call-done = bf16[1024,1024]{1,0:T(8,128)(2,1)} async-done(((bf16[256,1024]{1,0:T(8,128)(2,1)}), bf16[1024,1024]{1,0:T(8,128)(2,1)}) %all-gather.27.cloned.1.call-update) | async-done | bytes 2097168 | tf_op jit(solution)/shard_map/all_gather | solution.py:60
  547.3 44.6 %reduce-scatter.21.cloned.1.call-done = f32[256,1024]{1,0:T(8,128)} async-done(((f32[1024,1024]{1,0:T(8,128)}), f32[256,1024]{1,0:T(8,128)}) %reduce-scatter.21.cloned.1.call-update) | async-done | bytes 1048592 | tf_op jit(solution)/shard_map/reduce_scatter | solution.py:65
  596.4 22.2 %all-gather.29.cloned.1.call-done = bf16[1024,1024]{1,0:T(8,128)(2,1)} async-done(((bf16[256,1024]{1,0:T(8,128)(2,1)}), bf16[1024,1024]{1,0:T(8,128)(2,1)}) %all-gather.29.cloned.1.call-update) | async-done | bytes 2097168 | tf_op jit(solution)/shard_map/all_gather | solution.py:70
  631.1 44.6 %reduce-scatter.23.cloned.1.call-done = f32[256,1024]{1,0:T(8,128)} async-done(((f32[1024,1024]{1,0:T(8,128)}), f32[256,1024]{1,0:T(8,128)}) %reduce-scatter.23.cloned.1.call-update) | async-done | bytes 1048592 | tf_op jit(solution)/shard_map/reduce_scatter | solution.py:75
  681.8 22.7 %all-gather.31.cloned.1.call-done = bf16[1024,1024]{1,0:T(8,128)(2,1)} async-done(((bf16[256,1024]{1,0:T(8,128)(2,1)}), bf16[1024,1024]{1,0:T(8,128)(2,1)}) %all-gather.31.cloned.1.call-update) | async-done | bytes 2097168 | tf_op jit(solution)/shard_map/all_gather | solution.py:70
  704.5 11.4 multiply_reduce_fusion.6
  725.8 44.4 %reduce-scatter.25.cloned.1.call-done = f32[256,1024]{1,0:T(8,128)} async-done(((f32[1024,1024]{1,0:T(8,128)}), f32[256,1024]{1,0:T(8,128)}) %reduce-scatter.25.cloned.1.call-update) | async-done | bytes 1048592 | tf_op jit(solution)/shard_map/reduce_scatter | solution.py:75
  775.4 22.7 %all-gather.33.cloned.1.call-done = bf16[1024,1024]{1,0:T(8,128)(2,1)} async-done(((bf16[256,1024]{1,0:T(8,128)(2,1)}), bf16[1024,1024]{1,0:T(8,128)(2,1)}) %all-gather.33.cloned.1.call-update) | async-done | bytes 2097168 | tf_op jit(solution)/shard_map/all_gather | solution.py:70
  804.3 22.9 %while.29 = (s32[]{:T(128)}, f32[1024,4,64]{0,2,1:T(8,128)S(1)}, f32[1024,4,64]{0,2,1:T(8,128)}, bf16[2,512,4,64]{1,3,2,0:T(8,128)(2,1)}, bf16[2,512,4,64]{1,3,2...) while((s32[]{:T(128)}, f32[1024,4,64]{0,2,1:T(8,128)S(1)}, ...), condition=%wide.region_28.29_spmd.clone, body=%wide.region_26.28_spmd.clone.sunk | while | flops 1375075328 | bytes 82899216 | solution.py:153
  837.9 44.2 %reduce-scatter.27.cloned.1.call-done = f32[256,1024]{1,0:T(8,128)} async-done(((f32[1024,1024]{1,0:T(8,128)}), f32[256,1024]{1,0:T(8,128)}) %reduce-scatter.27.cloned.1.call-update) | async-done | bytes 1048592 | tf_op jit(solution)/shard_map/reduce_scatter | solution.py:75
  981.9 67.3 %reduce-scatter.39.cloned.1.call-done = f32[2,128,256]{2,1,0:T(8,128)} async-done(((f32[2,1024,256]{2,1,0:T(8,128)}), f32[2,128,256]{2,1,0:T(8,128)}) %reduce-scatter.39.cloned.1.call-update) | async-done | bytes 262160 | tf_op jit(solution)/shard_map/reduce_scatter | solution.py:377
  1053.2 63.4 %reduce-scatter.37.cloned.1.call-done = f32[256,128]{1,0:T(8,128)} async-done(((f32[256,1024]{1,0:T(8,128)}), f32[256,128]{1,0:T(8,128)}) %reduce-scatter.37.cloned.1.call-update) | async-done | bytes 131088 | tf_op jit(solution)/shard_map/reduce_scatter | solution.py:376
  1120.4 74.4 %reduce-scatter.35.cloned.1.call-done = f32[3,128,256]{1,2,0:T(8,128)} async-done(((f32[3,1024,256]{1,2,0:T(8,128)}), f32[3,128,256]{1,2,0:T(8,128)}) %reduce-scatter.35.cloned.1.call-update) | async-done | bytes 393232 | tf_op jit(solution)/shard_map/reduce_scatter | solution.py:375
  1203.9 37.0 %reduce-scatter.29.cloned.1.call-done = f32[256,1024]{1,0:T(8,128)} async-done(((f32[1024,1024]{1,0:T(8,128)}), f32[256,1024]{1,0:T(8,128)}) %reduce-scatter.29.cloned.1.call-update) | async-done | bytes 1048592 | tf_op jit(solution)/shard_map/reduce_scatter | solution.py:75
  1242.7 39.7 %all-reduce.3 = (f32[31,256]{1,0:T(8,128)S(1)}, f32[5,1024]{1,0:T(8,128)S(1)}) all-reduce(f32[31,256]{1,0:T(8,128)S(1)} %stack.272, f32[5,1024]{1,0:T(8,128)S(1)} %stack.278), channel_id=1, replica_groups=mesh['dp'=8,'tensor'=4] {'dp'}, use_global_device_ids=true, to_apply=%region_85.86 | all-reduce | flops 13056 | bytes 104448 | tf_op jit(solution)/shard_map/psum | solution.py:381
  1286.5 11.3 psum.38
  1302.6 92.7 %reduce-scatter.33.cloned.1.call-done = f32[2,1024,128]{2,1,0:T(8,128)} async-done(((f32[2,1024,1024]{2,1,0:T(8,128)}), f32[2,1024,128]{2,1,0:T(8,128)}) %reduce-scatter.33.cloned.1.call-update) | async-done | bytes 1048592 | tf_op jit(solution)/shard_map/reduce_scatter | solution.py:374
  1400.9 146.9 %reduce-scatter.31.cloned.1.call-done = f32[2,128,1024]{2,1,0:T(8,128)} async-done(((f32[2,1024,1024]{2,1,0:T(8,128)}), f32[2,128,1024]{2,1,0:T(8,128)}) %reduce-scatter.31.cloned.1.call-update) | async-done | bytes 1048592 | tf_op jit(solution)/shard_map/reduce_scatter | solution.py:373
  1557.9 39.1 %all-reduce.2 = (f32[17]{0:T(128)S(1)}, f32[17]{0:T(128)S(1)}) all-reduce(f32[17]{0:T(128)S(1)} %concatenate.9, f32[17]{0:T(128)S(1)} %concatenate.8), channel_id=1, replica_groups=mesh['dp'=8,'tensor'=4] {'dp','tensor'}, use_global_device_ids=true, to_apply=%region_97.98 | all-reduce | flops 34 | bytes 272 | tf_op jit(solution)/shard_map/psum | solution.py:415
  (419 shorter events, 331.3 us)
Async XLA Ops:
  7.2 31.6 %all-gather.13.cloned.1.call-start = ((), (), s32[]{:S(2)}) async-start(), calls=%async_computation.14 | async-start | bytes 2621440 | tf_op jit(solution)/shard_map/all_gather | solution.py:60
  13.4 101.6 %all-gather.15.cloned.1.call-start = ((), (), s32[]{:S(2)}) async-start(), calls=%async_computation.15 | async-start | bytes 4718592 | tf_op jit(solution)/shard_map/all_gather | solution.py:302
  15.5 175.4 %all-gather.17.cloned.1.call-start = ((), (), s32[]{:S(2)}) async-start(), calls=%async_computation.16 | async-start | bytes 4718592 | tf_op jit(solution)/shard_map/all_gather | solution.py:303
  17.7 223.3 %reduce-scatter.15.cloned.1.call-start = ((), (), s32[]{:S(2)}) async-start(), calls=%async_computation.17 | async-start | bytes 5242880 | tf_op jit(solution)/shard_map/reduce_scatter | solution.py:65
  198.1 93.9 %all-gather.21.cloned.1.call-start = ((), (), s32[]{:S(2)}) async-start(), calls=%async_computation.19 | async-start | bytes 1769472 | tf_op jit(solution)/shard_map/all_gather | solution.py:304
  201.6 113.3 %all-gather.19.cloned.1.call-start = ((), (), s32[]{:S(2)}) async-start(), calls=%async_computation.18 | async-start | bytes 2621440 | tf_op jit(solution)/shard_map/all_gather | solution.py:60
  243.8 140.0 %reduce-scatter.17.cloned.1.call-start = ((), (), s32[]{:S(2)}) async-start(), calls=%async_computation.20 | async-start | bytes 5242880 | tf_op jit(solution)/shard_map/reduce_scatter | solution.py:65
  339.2 90.0 %all-gather.25.cloned.1.call-start = ((), (), s32[]{:S(2)}) async-start(), calls=%async_computation.22 | async-start | bytes 1179648 | tf_op jit(solution)/shard_map/all_gather | solution.py:306
  340.9 111.8 %all-gather.23.cloned.1.call-start = ((), (), s32[]{:S(2)}) async-start(), calls=%async_computation.21 | async-start | bytes 2621440 | tf_op jit(solution)/shard_map/all_gather | solution.py:60
  386.5 124.2 %reduce-scatter.19.cloned.1.call-start = ((), (), s32[]{:S(2)}) async-start(), calls=%async_computation.23 | async-start | bytes 5242880 | tf_op jit(solution)/shard_map/reduce_scatter | solution.py:65
  387.2 328.6 %copy-start.54 = (f32[1024]{0:T(1024)}, f32[1024]{0:T(1024)S(1)}, u32[]{:S(2)}) copy-start(f32[1024]{0:T(1024)S(1)} %fusion.157) | copy-start | bytes 12292
  466.1 70.1 %all-gather.27.cloned.1.call-start = ((), (), s32[]{:S(2)}) async-start(), calls=%async_computation.24 | async-start | bytes 2621440 | tf_op jit(solution)/shard_map/all_gather | solution.py:60
  513.5 78.4 %reduce-scatter.21.cloned.1.call-start = ((), (), s32[]{:S(2)}) async-start(), calls=%async_computation.25 | async-start | bytes 5242880 | tf_op jit(solution)/shard_map/reduce_scatter | solution.py:65
  547.2 71.5 %all-gather.29.cloned.1.call-start = ((), (), s32[]{:S(2)}) async-start(), calls=%async_computation.26 | async-start | bytes 2621440 | tf_op jit(solution)/shard_map/all_gather | solution.py:70
  595.9 79.8 %reduce-scatter.23.cloned.1.call-start = ((), (), s32[]{:S(2)}) async-start(), calls=%async_computation.27 | async-start | bytes 5242880 | tf_op jit(solution)/shard_map/reduce_scatter | solution.py:75
  631.1 73.4 %all-gather.31.cloned.1.call-start = ((), (), s32[]{:S(2)}) async-start(), calls=%async_computation.28 | async-start | bytes 2621440 | tf_op jit(solution)/shard_map/all_gather | solution.py:70
  681.8 88.4 %reduce-scatter.25.cloned.1.call-start = ((), (), s32[]{:S(2)}) async-start(), calls=%async_computation.29 | async-start | bytes 5242880 | tf_op jit(solution)/shard_map/reduce_scatter | solution.py:75
  725.5 72.5 %all-gather.33.cloned.1.call-start = ((), (), s32[]{:S(2)}) async-start(), calls=%async_computation.30 | async-start | bytes 2621440 | tf_op jit(solution)/shard_map/all_gather | solution.py:70
  775.3 106.8 %reduce-scatter.27.cloned.1.call-start = ((), (), s32[]{:S(2)}) async-start(), calls=%async_computation.31 | async-start | bytes 5242880 | tf_op jit(solution)/shard_map/reduce_scatter | solution.py:75
  837.4 72.0 %all-gather.35.cloned.1.call-start = ((), (), s32[]{:S(2)}) async-start(), calls=%async_computation.32 | async-start | bytes 2621440 | tf_op jit(solution)/shard_map/all_gather | solution.py:70
  886.6 91.5 %reduce-scatter.41.cloned.1.call-start = ((), (), s32[]{:S(2)}) async-start(), calls=%async_computation.39 | async-start | bytes 1179648 | tf_op jit(solution)/shard_map/reduce_scatter | solution.py:378
  890.0 159.1 %reduce-scatter.39.cloned.1.call-start = ((), (), s32[]{:S(2)}) async-start(), calls=%async_computation.38 | async-start | bytes 2359296 | tf_op jit(solution)/shard_map/reduce_scatter | solution.py:377
  894.8 221.8 %reduce-scatter.37.cloned.1.call-start = ((), (), s32[]{:S(2)}) async-start(), calls=%async_computation.37 | async-start | bytes 1179648 | tf_op jit(solution)/shard_map/reduce_scatter | solution.py:376
  896.6 298.2 %reduce-scatter.35.cloned.1.call-start = ((), (), s32[]{:S(2)}) async-start(), calls=%async_computation.36 | async-start | bytes 3538944 | tf_op jit(solution)/shard_map/reduce_scatter | solution.py:375
  902.1 338.8 %reduce-scatter.29.cloned.1.call-start = ((), (), s32[]{:S(2)}) async-start(), calls=%async_computation.33 | async-start | bytes 5242880 | tf_op jit(solution)/shard_map/reduce_scatter | solution.py:75
  921.8 473.6 %reduce-scatter.33.cloned.1.call-start = ((), (), s32[]{:S(2)}) async-start(), calls=%async_computation.35 | async-start | bytes 9437184 | tf_op jit(solution)/shard_map/reduce_scatter | solution.py:374
  934.7 613.1 %reduce-scatter.31.cloned.1.call-start = ((), (), s32[]{:S(2)}) async-start(), calls=%async_computation.34 | async-start | bytes 9437184 | tf_op jit(solution)/shard_map/reduce_scatter | solution.py:373
  974.8 266.2 %copy-start.9 = (bf16[256,1024]{1,0:T(8,128)(2,1)S(1)}, bf16[256,1024]{1,0:T(8,128)(2,1)}, u32[]{:S(2)}) copy-start(bf16[256,1024]{1,0:T(8,128)(2,1)} %param.33) | copy-start | bytes 1572868
  974.8 266.2 %copy-start.51 = (f32[1,1,1024]{2,0,1:T(1,128)S(1)}, f32[1,1,1024]{2,0,1:T(1,128)}, u32[]{:S(2)}) copy-start(f32[1,1,1024]{2,0,1:T(1,128)} %copy-done.50) | copy-start | bytes 12292
  974.8 266.2 %copy-start.58 = (f32[256]{0:T(256)S(1)}, f32[256]{0:T(256)}, u32[]{:S(2)}) copy-start(f32[256]{0:T(256)} %copy-done.57) | copy-start | bytes 3076
  974.8 266.1 %copy-start.67 = (f32[256]{0:T(256)S(1)}, f32[256]{0:T(256)}, u32[]{:S(2)}) copy-start(f32[256]{0:T(256)} %copy-done.66) | copy-start | bytes 3076
  1053.2 342.2 %copy-start.12 = (f32[2,2,1024,128]{3,2,1,0:T(8,128)S(1)}, f32[2,2,1024,128]{3,2,1,0:T(8,128)}, u32[]{:S(2)}) copy-start(f32[2,2,1024,128]{3,2,1,0:T(8,128)} %param.41) | copy-start | bytes 6291460
  (81 other events, 3851.0 us)
Sparse Core Ops, SparseCore 0:
  13.5 25.2 all-gather.12
  41.6 73.3 all-gather.14
  117.6 73.2 all-gather.16
  198.3 42.6 reduce-scatter.14
  243.6 48.3 all-gather.20
  294.1 20.7 all-gather.18
  339.3 44.4 reduce-scatter.16
  386.6 42.5 all-gather.24
  431.3 21.3 all-gather.22
  466.2 44.4 reduce-scatter.18
  513.6 22.5 all-gather.26
  547.3 44.4 reduce-scatter.20
  596.0 22.5 all-gather.28
  631.2 44.4 reduce-scatter.22
  681.9 22.5 all-gather.30
  725.7 44.4 reduce-scatter.24
  775.4 22.5 all-gather.32
  837.5 44.4 reduce-scatter.26
  886.7 22.6 all-gather.34
  914.2 63.8 reduce-scatter.40
  982.2 66.8 reduce-scatter.38
  1053.7 62.8 reduce-scatter.36
  1120.6 74.0 reduce-scatter.34
  1197.3 43.6 reduce-scatter.28
  1245.1 150.1 reduce-scatter.32
  1399.8 147.9 reduce-scatter.30
where the time goes:
time: 1640 us
  waiting for transfers between devices  1130 us (69%)
  blocking collectives  150 us (9%)
  other arithmetic  135 us (8%)
  matrix products  135 us (8%)
  local copies, waits for them, and re-layouts  59.2 us (4%)
  between operations  25.6 us (2%)
    reduce_scatter x4, waiting for transfers between devices, leave_rows(): lax.psum_scatter(partial_sum, 'tensor', scatter_dimension=0, tiled=True)  171 us
    reduce_scatter x4, waiting for transfers between devices, leave_grads(): lax.psum_scatter(partial_sum, 'tensor', scatter_dimension=0, tiled=True)  170 us
    reduce_scatter x1, waiting for transfers between devices, shards(): lax.psum_scatter(expand_grad, 'dp', scatter_dimension=1, tiled=True)  147 us
    reduce_scatter x1, waiting for transfers between devices, shards(): lax.psum_scatter(shrink_grad, 'dp', scatter_dimension=2, tiled=True)  92.7 us
    all_gather x4, waiting for transfers between devices, enter_rows(): lax.all_gather(normed.astype(jnp.bfloat16), 'tensor', axis=0, tiled=True)  90.2 us
    all_gather x1, waiting for transfers between devices, shards(): lax.all_gather(expand_params[0].astype(jnp.bfloat16), 'dp', axis=1, tiled...  76.2 us
    all_gather x4, waiting for transfers between devices, enter_grads(): lax.all_gather(upstream.astype(jnp.bfloat16), 'tensor', axis=0, tiled=True)  74.8 us
    reduce_scatter x1, waiting for transfers between devices, shards(): lax.psum_scatter(project_grad, 'dp', scatter_dimension=1, tiled=True)  74.4 us
  transfers between devices with their start and end apart: 26, of which 26 were waited for; matrix products, arithmetic and copies ran while one was open for 8% of the time, Pallas kernels for 0%

commit v1 on v0

v1 whole, which is shorter than its diff:
```python
import functools
import math
from types import SimpleNamespace

import jax
import jax.numpy as jnp
from jax import lax
from jax.experimental import pallas as pl
from jax.experimental.pallas import tpu as pltpu
from jax.sharding import PartitionSpec as P

HEAD_DIM = 64
KERNEL = 31
BLOCK = 512

EPSILON = 1e-05
ADAM_EPS = 1e-06
DECAY_RATE = 0.01
MASKED = -1000000000.0

F32 = jnp.float32
BF16 = jnp.bfloat16
MESH = pl.DeviceIdType.MESH
STEP = 16
TILE = 256
GRANT = 50 * 1024 * 1024


class Spot:
    def __init__(self, dims):
        self.dims = dims
        self.d = lax.axis_index("dp")
        self.t = lax.axis_index("tensor")
        self.y = lax.div(self.t, 2)
        self.c = lax.rem(self.t, 2)
        self.a = lax.div(self.d, dims.nb)
        self.b = lax.rem(self.d, dims.nb)

    def sibling(self):
        return (self.d, self.y * 2 + 1 - self.c)

    def across(self, j):
        return (self.d, lax.rem(self.y + j, self.dims.ny) * 2 + self.c)

    def slow(self, j):
        return (lax.rem(self.a + j, self.dims.na) * self.dims.nb + self.b, self.t)

    def fast(self, j):
        return (self.a * self.dims.nb + lax.rem(self.b + j, self.dims.nb), self.t)

    def tensor_peers(self):
        return [self.sibling()] + [self.across(j) for j in range(1, self.dims.ny)]

    def data_peers(self):
        return [self.slow(j) for j in range(1, self.dims.na)] + [
            self.fast(j) for j in range(1, self.dims.nb)
        ]


def greet(peers):
    barrier = pltpu.get_barrier_semaphore()
    for peer in peers:
        pl.semaphore_signal(barrier, 1, device_id=peer, device_id_type=MESH)
    pl.semaphore_wait(barrier, len(peers))


def remote(source, target, send, recv, peer):
    return pltpu.make_async_remote_copy(
        src_ref=source,
        dst_ref=target,
        send_sem=send,
        recv_sem=recv,
        device_id=peer,
        device_id_type=MESH,
    )


def loop(count, body, unroll=1):
    def step(i, carry):
        body(i)
        return carry

    lax.fori_loop(0, count, step, 0, unroll=unroll)


def rows_of(i, step=STEP):
    return pl.ds(pl.multiple_of(i * step, step), step)


def call(body, ins, outs, scratch, cid, flops=0, moved=0):
    in_names, out_names, scratch_names = list(ins), list(outs), list(scratch)

    def kernel(*refs):
        names = in_names + out_names + scratch_names
        body(SimpleNamespace(**dict(zip(names, refs))))

    results = pl.pallas_call(
        kernel,
        out_shape=[jax.ShapeDtypeStruct(shape, kind) for shape, kind, _ in outs.values()],
        in_specs=[pl.BlockSpec(memory_space=space) for _, space in ins.values()],
        out_specs=[pl.BlockSpec(memory_space=space) for _, _, space in outs.values()],
        scratch_shapes=list(scratch.values()),
        compiler_params=pltpu.CompilerParams(
            collective_id=cid, has_side_effects=cid is not None, vmem_limit_bytes=GRANT
        ),
        cost_estimate=pl.CostEstimate(flops=flops, bytes_accessed=moved, transcendentals=0),
    )(*[array for array, _ in ins.values()])
    return dict(zip(out_names, results))


VM = pltpu.VMEM
HB = pl.ANY
SM = pltpu.SMEM
SEMS = pltpu.SemaphoreType.DMA


def tagged(prefix, tag, specs):
    return {prefix + name + tag: spec for name, spec in specs.items()}


def bound(refs, prefix, tag, specs):
    return SimpleNamespace(**{name: getattr(refs, prefix + name + tag) for name in specs})


class Gather:
    def __init__(self, tag, dims):
        self.tag, self.dims = tag, dims
        na, nb = dims.na, dims.nb
        m, k = max(nb - 1, 1), max(na - 1, 1)
        self.specs = dict(
            loc=SEMS,
            xs=SEMS((m,)),
            xr=SEMS((m,)),
            us=SEMS((k,)),
            ur=SEMS((k,)),
            ds=SEMS((k,)),
            dr=SEMS((k,)),
            fs=SEMS((2, k, m)),
            fr=SEMS((2, k, m)),
        )
        self.stage = 0

    def scratch(self):
        return tagged("g", self.tag, self.specs)

    def bind(self, refs, spot, source, whole):
        self.sem = bound(refs, "g", self.tag, self.specs)
        self.spot, self.source, self.whole = spot, source, whole
        return self

    def rows(self, d):
        shard = self.source.shape[0]
        return self.whole.at[pl.ds(pl.multiple_of(d * shard, shard), shard)]

    def block(self, a):
        return self.rows(a * self.dims.nb + self.spot.b)

    def hop(self, way, s):
        spot, sem = self.spot, self.sem
        step = 1 if way == 0 else -1
        target = self.block(spot.a - step * (s - 1))
        source = self.source if s == 1 else target
        send, recv = (sem.us, sem.ur) if way == 0 else (sem.ds, sem.dr)
        peer = ((spot.a + step) * self.dims.nb + spot.b, spot.t)
        return remote(source, target, send.at[s - 1], recv.at[s - 1], peer)

    def sends(self, way, s):
        spot, na = self.spot, self.dims.na
        if way == 0:
            return jnp.logical_and(spot.a - (s - 1) >= 0, spot.a + 1 < na)
        return jnp.logical_and(spot.a + (s - 1) < na, spot.a - 1 >= 0)

    def has(self, way, s):
        return self.spot.a - s >= 0 if way == 0 else self.spot.a + s < self.dims.na

    def hand(self, way, s, i):
        block = self.block(self.spot.a - s if way == 0 else self.spot.a + s)
        sem = self.sem
        return remote(
            block, block, sem.fs.at[way, s - 1, i - 1], sem.fr.at[way, s - 1, i - 1], self.spot.fast(i)
        )

    def start(self):
        spot, dims, sem = self.spot, self.dims, self.sem
        mine = self.rows(spot.d)
        if dims.na > 1:
            for way in range(2):

                @pl.when(self.sends(way, 1))
                def _(way=way):
                    self.hop(way, 1).start()

        self.own = [
            remote(self.source, mine, sem.xs.at[j - 1], sem.xr.at[j - 1], spot.fast(j))
            for j in range(1, dims.nb)
        ]
        for copy in self.own:
            copy.start()
        self.local = pltpu.make_async_copy(self.source, mine, sem.loc)
        self.local.start()

    def advance(self):
        dims = self.dims
        self.stage += 1
        s = self.stage
        if s >= dims.na:
            return False
        for way in range(2):

            @pl.when(self.has(way, s))
            def _(way=way):
                self.hop(way, s).wait_recv()
                for i in range(1, dims.nb):
                    self.hand(way, s, i).start()

            if s + 1 < dims.na:

                @pl.when(self.sends(way, s + 1))
                def _(way=way):
                    self.hop(way, s + 1).start()

        return True

    def finish(self):
        dims = self.dims
        while self.advance():
            pass
        self.local.wait()
        for copy in self.own:
            copy.wait()
        for s in range(1, dims.na):
            for way in range(2):

                @pl.when(self.sends(way, s))
                def _(way=way, s=s):
                    self.hop(way, s).wait_send()

                @pl.when(self.has(way, s))
                def _(way=way, s=s):
                    for i in range(1, dims.nb):
                        self.hand(way, s, i).wait()


class Scatter:
    def __init__(self, tag, dims, rows, first, columns):
        self.tag, self.dims, self.size = tag, dims, (rows, columns)
        self.columns = pl.ds(first, columns)
        na, nb = dims.na, dims.nb
        m, k = max(nb - 1, 1), max(na - 1, 1)
        self.specs = dict(
            held=VM((na, rows, columns), BF16),
            one=VM((m, na, rows, columns), BF16),
            two=VM((k, rows, columns), BF16),
            loc=SEMS,
            xs=SEMS((m,)),
            xr=SEMS((m,)),
            zs=SEMS((k,)),
            zr=SEMS((k,)),
        )
        self.stage = 0

    def scratch(self):
        return tagged("s", self.tag, self.specs)

    def bind(self, refs, spot, source, result):
        self.r = bound(refs, "s", self.tag, self.specs)
        self.spot, self.source, self.result = spot, source, result
        return self

    def start(self):
        spot, dims, r = self.spot, self.dims, self.r
        self.first = []
        for j in range(1, dims.nb):
            block = lax.rem(spot.b + j, dims.nb)
            copy = remote(
                self.source.at[:, block, :, self.columns],
                r.one.at[j - 1],
                r.xs.at[j - 1],
                r.xr.at[j - 1],
                spot.fast(j),
            )
            copy.start()
            self.first.append(copy)
        self.local = pltpu.make_async_copy(
            self.source.at[:, spot.b, :, self.columns], r.held, r.loc
        )
        self.local.start()

    def advance(self):
        if self.stage:
            return False
        self.stage = 1
        spot, dims, r = self.spot, self.dims, self.r
        rows, columns = self.size
        self.local.wait()
        for copy in self.first:
            copy.wait_recv()
        if dims.nb > 1:
            for a in range(dims.na):

                def add(i, a=a):
                    rs = rows_of(i)
                    total = r.held[a, rs, :].astype(F32)
                    for j in range(dims.nb - 1):
                        total = total + r.one[j, a, rs, :].astype(F32)
                    r.held[a, rs, :] = total.astype(BF16)

                loop(rows // STEP, add, 2)
        self.second = []
        for j in range(1, dims.na):
            copy = remote(
                r.held.at[lax.rem(spot.a + j, dims.na)],
                r.two.at[j - 1],
                r.zs.at[j - 1],
                r.zr.at[j - 1],
                spot.slow(j),
            )
            copy.start()
            self.second.append(copy)
        return True

    def finish(self):
        self.advance()
        dims, r = self.dims, self.r
        rows, columns = self.size
        for copy in self.second:
            copy.wait_recv()

        def add(i):
            rs = rows_of(i)
            total = r.held[self.spot.a, rs, :].astype(F32)
            for j in range(dims.na - 1):
                total = total + r.two[j, rs, :].astype(F32)
            self.result[rs, self.columns] = total

        loop(rows // STEP, add, 2)
        for copy in self.first + self.second:
            copy.wait_send()


class Edge:
    def __init__(self, dims, gather=True, owner_only=False):
        self.dims, self.gather, self.owner_only = dims, gather, owner_only

    def scratch(self):
        ny, L, D = self.dims.ny, self.dims.L, self.dims.D
        m = max(ny - 1, 1)
        return dict(
            e_own=VM((ny, L, D), F32),
            e_give=VM((ny, L, D), BF16),
            e_take=VM((ny, L, D), BF16),
            e_sum=VM((ny, L, D), BF16),
            e_far=VM((m, ny, L, D), BF16),
            e_ds=SEMS((ny,)),
            e_dr=SEMS((ny,)),
            e_ys=SEMS((m, ny)),
            e_yr=SEMS((m, ny)),
            e_ns=SEMS((ny,)),
            e_nr=SEMS((ny,)),
        )

    def bind(self, refs, spot, normed=None):
        self.refs, self.spot, self.normed = refs, spot, normed
        self.near, self.far, self.handed = {}, {}, {}
        return self

    def put(self, k, columns, part):
        L, refs = self.dims.L, self.refs
        low, high = part[:L], part[L:]
        first = self.spot.c == 0
        refs.e_own[k, :, columns] = jnp.where(first, low, high)
        refs.e_give[k, :, columns] = jnp.where(first, high, low).astype(BF16)

    def start(self, k):
        refs = self.refs
        copy = remote(
            refs.e_give.at[k], refs.e_take.at[k], refs.e_ds.at[k], refs.e_dr.at[k], self.spot.sibling()
        )
        copy.start()
        self.near[k] = copy

    def cross(self, k):
        refs, dims = self.refs, self.dims
        self.near[k].wait_recv()

        def add(i):
            rs = rows_of(i)
            total = refs.e_own[k, rs, :] + refs.e_take[k, rs, :].astype(F32)
            refs.e_own[k, rs, :] = total
            refs.e_sum[k, rs, :] = total.astype(BF16)

        loop(dims.L // STEP, add, 2)
        if not self.owner_only:
            self.far[k] = []
            for j in range(1, dims.ny):
                copy = remote(
                    refs.e_sum.at[k],
                    refs.e_far.at[j - 1, k],
                    refs.e_ys.at[j - 1, k],
                    refs.e_yr.at[j - 1, k],
                    self.spot.across(j),
                )
                copy.start()
                self.far[k].append(copy)

    def cross_owner(self):
        refs, dims = self.refs, self.dims
        copies = []
        for j in range(1, dims.ny):
            copy = remote(
                refs.e_sum.at[lax.rem(self.spot.y + j, dims.ny)],
                refs.e_far.at[j - 1, 0],
                refs.e_ys.at[j - 1, 0],
                refs.e_yr.at[j - 1, 0],
                self.spot.across(j),
            )
            copy.start()
            copies.append(copy)
        self.far[0] = copies

    def total(self, k, rs, slot=None):
        refs = self.refs
        total = refs.e_own[k, rs, :]
        for j in range(self.dims.ny - 1):
            total = total + refs.e_far[j, k if slot is None else slot, rs, :].astype(F32)
        return total

    def settle(self, k, row_fn):
        refs, dims, spot = self.refs, self.dims, self.spot
        for copy in self.far[k]:
            copy.wait_recv()
        base = (k * 2 + spot.c) * dims.L

        def body(i):
            rs = rows_of(i)
            rows = row_fn(self.total(k, rs), k, rs)
            if self.gather:
                target = pl.ds(pl.multiple_of(base + i * STEP, STEP), STEP)
                self.normed[target, :] = rows

        loop(dims.L // STEP, body, 2)
        if self.gather:
            block = self.normed.at[pl.ds(pl.multiple_of(base, dims.L), dims.L)]
            copy = remote(block, block, refs.e_ns.at[k], refs.e_nr.at[k], spot.sibling())
            copy.start()
            self.handed[k] = copy

    def arrived(self, k):
        self.handed[k].wait_recv()

    def drain(self):
        for copy in self.near.values():
            copy.wait_send()
        for copies in self.far.values():
            for copy in copies:
                copy.wait_send()
        for copy in self.handed.values():
            copy.wait_send()


def unit(hidden):
    center = hidden - jnp.mean(hidden, axis=-1, keepdims=True)
    spread = jnp.mean(center * center, axis=-1, keepdims=True)
    inverse = lax.rsqrt(spread + EPSILON)
    return center * inverse, inverse


def unit_back(upstream, xhat, inverse, gain):
    scaled = upstream * gain
    return inverse * (
        scaled
        - jnp.mean(scaled, axis=-1, keepdims=True)
        - xhat * jnp.mean(scaled * xhat, axis=-1, keepdims=True)
    )


def fold(rows):
    return rows[:8] + rows[8:]


def head_kernel(dims, cid, frames, cotangent, gain, expand_shard, shrink_shard):
    ny, L, D = dims.ny, dims.L, dims.D
    beside = Beside(dims, [expand_shard, shrink_shard])
    m = max(ny - 1, 1)
    scratch = dict(
        xs=SEMS((m,)), xr=SEMS((m,)), os=SEMS((m,)), orr=SEMS((m,)), ns=SEMS((ny,)), nr=SEMS((ny,))
    )

    def body(r):
        spot = Spot(dims)
        greet(spot.tensor_peers() + spot.data_peers())
        beside.start(r, spot)
        moves = []
        for j in range(1, ny):
            copy = remote(r.x, r.xh.at[spot.y], r.xs.at[j - 1], r.xr.at[j - 1], spot.across(j))
            copy.start()
            other = remote(r.og, r.ogh.at[spot.y], r.os.at[j - 1], r.orr.at[j - 1], spot.across(j))
            other.start()
            moves.append((copy, other))

        def own_rows(i):
            rs = rows_of(i)
            r.xh[spot.y, rs, :] = r.x[rs, :]
            r.ogh[spot.y, rs, :] = r.og[rs, :]

        loop(L // STEP, own_rows)
        handed = []

        def normalize(y, slot):
            base = (y * 2 + spot.c) * L

            def rows(i):
                xhat, _ = unit(r.xh[y, rows_of(i), :].astype(F32))
                target = pl.ds(pl.multiple_of(base + i * STEP, STEP), STEP)
                r.n[target, :] = (xhat * r.g[...]).astype(BF16)

            loop(L // STEP, rows, 2)
            block = r.n.at[pl.ds(pl.multiple_of(base, L), L)]
            copy = remote(block, block, r.ns.at[slot], r.nr.at[slot], spot.sibling())
            copy.start()
            handed.append(copy)

        normalize(spot.y, 0)
        for j in range(1, ny):
            moves[j - 1][0].wait_recv()
            normalize(lax.rem(spot.y + ny - j, ny), j)
        beside.advance()
        for copy in handed:
            copy.wait()
        for copy, other in moves:
            copy.wait_send()
            other.wait()
        beside.finish()

    return call(
        body,
        dict(
            x=(frames, VM),
            og=(cotangent, VM),
            g=(gain, VM),
        )
        | beside.ins(),
        dict(
            xh=((ny, L, D), BF16, VM),
            ogh=((ny, L, D), BF16, VM),
            n=((dims.S, D), BF16, VM),
        )
        | beside.outs(),
        scratch | beside.scratch(),
        cid,
    )


class Beside:
    def __init__(self, dims, gathers=(), scatters=(), pieces=2):
        self.dims = dims
        self.arrays = list(gathers) + list(scatters)
        self.gathers = len(gathers)
        self.jobs = [(i, Gather(str(i), dims)) for i in range(len(gathers))]
        for i, source in enumerate(scatters):
            rows, width = source.shape[2:]
            count = pieces if width % (pieces * 128) == 0 else 1
            for piece in range(count):
                tag = str(len(self.jobs))
                part = width // count
                self.jobs.append(
                    (self.gathers + i, Scatter(tag, dims, rows, piece * part, part))
                )

    def peers(self, spot):
        return spot.data_peers() if self.jobs else []

    def ins(self):
        return {"bi" + str(i): (source, HB) for i, source in enumerate(self.arrays)}

    def outs(self):
        named = {}
        for i, source in enumerate(self.arrays):
            if i < self.gathers:
                rows, columns = source.shape
                shape = ((rows * self.dims.na * self.dims.nb, columns), BF16, HB)
            else:
                shape = (source.shape[2:], F32, VM)
            named["bo" + str(i)] = shape
        return named

    def scratch(self):
        named = {}
        for _, job in self.jobs:
            named |= job.scratch()
        return named

    def start(self, refs, spot):
        for i, job in self.jobs:
            job.bind(refs, spot, getattr(refs, "bi" + str(i)), getattr(refs, "bo" + str(i))).start()

    def advance(self):
        for _, job in self.jobs:
            job.advance()

    def finish(self):
        for _, job in self.jobs:
            job.finish()


def up_products(r, dims, k):
    m = 2 * dims.L

    def column(j):
        rows, cs = pl.ds(k * m, m), rows_of(j, TILE)
        before = jnp.dot(r.n[rows, :], r.e[:, cs], preferred_element_type=F32)
        gate = jax.nn.sigmoid(before)
        r.u[rows, cs] = (before * gate).astype(BF16)
        r.slope[rows, cs] = (gate * (1.0 + before * (1.0 - gate))).astype(BF16)

    loop(dims.F // TILE, column)


def down_products(edge, k, operand, matrix, dims, width):
    m = 2 * dims.L

    def column(j):
        cs = rows_of(j, TILE)
        part = lax.dot_general(
            operand[pl.ds(k * m, m), :],
            matrix[cs, :],
            (((1,), (1,)), ((), ())),
            preferred_element_type=F32,
        )
        edge.put(k, cs, part)

    loop(width // TILE, column)


def weight_product(result, rows_side, columns_side, dims):
    def block(i):
        cs = rows_of(i, TILE)
        result[cs, :] = lax.dot_general(
            rows_side[:, cs],
            columns_side[...],
            (((0,), (0,)), ((), ())),
            preferred_element_type=F32,
        ).astype(BF16)

    loop(dims.D // TILE, block)


def forward_rows(r, scale):
    def rows(total, k, rs):
        hidden = r.h[k, rs, :].astype(F32) + scale * total
        r.hn[k, rs, :] = hidden
        xhat, _ = unit(hidden)
        return (xhat * r.g[...]).astype(BF16)

    return rows


def backward_rows(r, scale, spot):
    def rows(total, k, rs):
        xhat, inverse = unit(r.h[k, rs, :].astype(F32))
        own = jnp.where(spot.y == k, 1.0, 0.0)
        r.dg[...] += fold(total * xhat) * own
        grad = r.gh[k, rs, :] + unit_back(total, xhat, inverse, r.g[...])
        r.ghn[k, rs, :] = grad
        return (scale * grad).astype(BF16)

    return rows


def ff_forward(dims, cid, normed, expand, shrink, hidden, gain, beside):
    ny, L, D, S, F = dims.ny, dims.L, dims.D, dims.S, dims.F
    edge = Edge(dims)

    def body(r):
        spot = Spot(dims)
        greet(spot.tensor_peers() + beside.peers(spot))
        beside.start(r, spot)
        edge.bind(r, spot, r.nn)
        for k in range(ny):
            up_products(r, dims, k)
            down_products(edge, k, r.u, r.rt, dims, D)
            edge.start(k)
            edge.cross(k)
        beside.advance()
        for k in range(ny):
            edge.settle(k, forward_rows(r, 0.5))
            beside.advance()
        for k in range(ny):
            edge.arrived(k)
        edge.drain()
        beside.finish()

    return call(
        body,
        dict(
            n=(normed, VM),
            e=(expand, VM),
            rt=(shrink, VM),
            h=(hidden, VM),
            g=(gain, VM),
        )
        | beside.ins(),
        dict(
            u=((S, F), BF16, VM),
            slope=((S, F), BF16, VM),
            hn=((ny, L, D), F32, VM),
            nn=((S, D), BF16, VM),
        )
        | beside.outs(),
        edge.scratch() | beside.scratch(),
        cid,
    )


def ff_turn(dims, cid, normed, expand, shrink, hidden, gain, cotangent, beside):
    ny, L, D, S, F = dims.ny, dims.L, dims.D, dims.S, dims.F
    edge = Edge(dims)

    def body(r):
        spot = Spot(dims)
        greet(spot.tensor_peers() + beside.peers(spot))
        beside.start(r, spot)
        edge.bind(r, spot, r.w)
        r.dg[...] = jnp.zeros_like(r.dg)

        def rows(total, k, rs):
            xhat, inverse = unit(r.h[k, rs, :] + 0.5 * total)
            r.fo[k, rs, :] = (xhat * r.g[...]).astype(BF16)
            upstream = r.og[k, rs, :].astype(F32)
            own = jnp.where(spot.y == k, 1.0, 0.0)
            r.dg[...] += fold(upstream * xhat) * own
            grad = unit_back(upstream, xhat, inverse, r.g[...])
            r.ghn[k, rs, :] = grad
            return (0.5 * grad).astype(BF16)

        for k in range(ny):
            up_products(r, dims, k)
            down_products(edge, k, r.u, r.rt, dims, D)
            edge.start(k)
            edge.cross(k)
        beside.advance()
        for k in range(ny):
            edge.settle(k, rows)
        for k in range(ny):
            edge.arrived(k)
        edge.drain()
        beside.finish()

    return call(
        body,
        dict(
            n=(normed, VM),
            e=(expand, VM),
            rt=(shrink, VM),
            h=(hidden, VM),
            g=(gain, VM),
            og=(cotangent, VM),
        )
        | beside.ins(),
        dict(
            u=((S, F), BF16, VM),
            slope=((S, F), BF16, VM),
            fo=((ny, L, D), BF16, VM),
            ghn=((ny, L, D), F32, VM),
            w=((S, D), BF16, VM),
            dg=((8, D), F32, VM),
        )
        | beside.outs(),
        edge.scratch() | beside.scratch(),
        cid,
    )


def ff_back(dims, cid, upstream, expand, shrink, slope, inner, normed, grad, hidden, gain, beside, last):
    ny, L, D, S, F = dims.ny, dims.L, dims.D, dims.S, dims.F
    edge = Edge(dims, gather=not last, owner_only=last)
    m = 2 * L

    def body(r):
        spot = Spot(dims)
        greet(spot.tensor_peers() + beside.peers(spot))
        beside.start(r, spot)
        edge.bind(r, spot, None if last else r.wn)
        r.dg[...] = jnp.zeros_like(r.dg)
        for k in range(ny):

            def column(j, k=k):
                rows, cs = pl.ds(k * m, m), rows_of(j, TILE)
                back = jnp.dot(r.w[rows, :], r.rt[:, cs], preferred_element_type=F32)
                r.db[rows, cs] = (back * r.slope[rows, cs].astype(F32)).astype(BF16)

            loop(F // TILE, column)
            down_products(edge, k, r.db, r.e, dims, D)
            edge.start(k)
            edge.cross(k)
        if last:
            edge.cross_owner()
        weight_product(r.de, r.n, r.db, dims)
        weight_product(r.dr, r.w, r.u, dims)
        beside.advance()
        if last:
            for copy in edge.far[0]:
                copy.wait_recv()

            def rows(i):
                rs = rows_of(i)
                total = edge.total(spot.y, rs, 0)
                xhat, inverse = unit(r.h[spot.y, rs, :].astype(F32))
                r.dg[...] += fold(total * xhat)
                back = r.gh[spot.y, rs, :] + unit_back(total, xhat, inverse, r.g[...])
                r.gin[rs, :] = back.astype(BF16)

            loop(L // STEP, rows, 2)
        else:
            for k in range(ny):
                edge.settle(k, backward_rows(r, 1.0, spot))
            for k in range(ny):
                edge.arrived(k)
        edge.drain()
        beside.finish()

    if last:
        outs = dict(gin=((L, D), BF16, VM))
    else:
        outs = dict(ghn=((ny, L, D), F32, VM), wn=((S, D), BF16, VM))
    return call(
        body,
        dict(
            w=(upstream, VM),
            e=(expand, VM),
            rt=(shrink, VM),
            slope=(slope, VM),
            u=(inner, VM),
            n=(normed, VM),
            gh=(grad, VM),
            h=(hidden, VM),
            g=(gain, VM),
        )
        | beside.ins(),
        outs
        | dict(
            de=((D, F), BF16, VM),
            dr=((D, F), BF16, VM),
            dg=((8, D), F32, VM),
        )
        | beside.outs(),
        dict(db=VM((S, F), BF16)) | edge.scratch() | beside.scratch(),
        cid,
    )


def edge_forward(dims, cid, part, hidden, gain, beside):
    ny, L, D, S = dims.ny, dims.L, dims.D, dims.S
    edge = Edge(dims)

    def body(r):
        spot = Spot(dims)
        greet(spot.tensor_peers() + beside.peers(spot))
        beside.start(r, spot)
        edge.bind(r, spot, r.nn)
        for k in range(ny):
            loop(
                D // TILE,
                lambda j, k=k: edge.put(
                    k, rows_of(j, TILE), r.p[pl.ds(k * 2 * L, 2 * L), rows_of(j, TILE)]
                ),
            )
            edge.start(k)
            edge.cross(k)
        beside.advance()
        for k in range(ny):
            edge.settle(k, forward_rows(r, 1.0))
            beside.advance()
        for k in range(ny):
            edge.arrived(k)
        edge.drain()
        beside.finish()

    return call(
        body,
        dict(p=(part, VM), h=(hidden, VM), g=(gain, VM)) | beside.ins(),
        dict(hn=((ny, L, D), F32, VM), nn=((S, D), BF16, VM)) | beside.outs(),
        edge.scratch() | beside.scratch(),
        cid,
    )


def edge_back(dims, cid, part, grad, hidden, gain, scale, beside):
    ny, L, D, S = dims.ny, dims.L, dims.D, dims.S
    edge = Edge(dims)

    def body(r):
        spot = Spot(dims)
        greet(spot.tensor_peers() + beside.peers(spot))
        beside.start(r, spot)
        edge.bind(r, spot, r.wn)
        r.dg[...] = jnp.zeros_like(r.dg)
        for k in range(ny):
            loop(
                D // TILE,
                lambda j, k=k: edge.put(
                    k, rows_of(j, TILE), r.p[pl.ds(k * 2 * L, 2 * L), rows_of(j, TILE)]
                ),
            )
            edge.start(k)
            edge.cross(k)
        beside.advance()
        for k in range(ny):
            edge.settle(k, backward_rows(r, scale, spot))
        for k in range(ny):
            edge.arrived(k)
        edge.drain()
        beside.finish()

    return call(
        body,
        dict(p=(part, VM), gh=(grad, VM), h=(hidden, VM), g=(gain, VM)) | beside.ins(),
        dict(
            ghn=((ny, L, D), F32, VM),
            wn=((S, D), BF16, VM),
            dg=((8, D), F32, VM),
        )
        | beside.outs(),
        edge.scratch() | beside.scratch(),
        cid,
    )


def direction_of(mean, square, master, rates, decay):
    return mean * rates[4] / (jnp.sqrt(square * rates[5]) + ADAM_EPS) + decay * master


def moments_of(grad, mean, square, rates):
    return (
        rates[0] * mean + (1.0 - rates[0]) * grad,
        rates[1] * square + (1.0 - rates[1]) * grad * grad,
    )


def tile_rows(shape):
    rows, columns = shape[-2:]
    step = min(rows, max(8, 16384 // max(columns, 128)))
    return step if rows % step == 0 and step % 8 == 0 else rows


def eighths(tile):
    rows, columns = tile.shape
    return tile.reshape(rows // 8, 8, columns).sum(axis=0) if rows % 8 == 0 else tile


def flip(result, source, dims):
    def part(j):
        cs = rows_of(j, 128)
        result[cs, :] = source[:, cs].T

    loop(source.shape[1] // 128, part)


PLACES = (0, 1, 2, 3, 4, 6, 5, 7)


def piece_rows(shapes):
    rows, total = {}, 0
    for i in PLACES:
        rows[i] = total
        total += shapes[i][0]
    return rows


class Relay:
    def __init__(self, tag, count, shape):
        self.tag, self.count = tag, count
        k = max(count - 1, 1)
        self.specs = dict(slots=VM((count,) + shape, F32), s=SEMS((k,)), r=SEMS((k,)))

    def scratch(self):
        return tagged("r", self.tag, self.specs)

    def start(self, refs, place, peers, value):
        self.r = bound(refs, "r", self.tag, self.specs)
        r = self.r
        r.slots[place] = value
        self.copies = []
        for j, peer in enumerate(peers):
            copy = remote(r.slots.at[place], r.slots.at[place], r.s.at[j], r.r.at[j], peer)
            copy.start()
            self.copies.append(copy)

    def finish(self):
        for copy in self.copies:
            copy.wait()
        total = self.r.slots[0]
        for i in range(1, self.count):
            total = total + self.r.slots[i]
        return total


def gradient_kernel(dims, cid, rates, entries, scatter, sums, gain_parts, kernel_part):
    D, F, H, C = dims.D, dims.F, dims.H, dims.C
    beside = Beside(dims, scatters=scatter)
    shard = scatter[0].shape[2]
    count_t, count_d = dims.ny * 2, dims.na * dims.nb
    gains_relays = [
        Relay("0", 2, (8, D)), Relay("1", dims.ny, (8, D)),
        Relay("2", dims.na, (8, D)), Relay("3", dims.nb, (8, D)),
    ]
    taps_relays = [Relay("4", dims.na, (KERNEL, C)), Relay("5", dims.nb, (KERNEL, C))]
    norm_relays = [Relay("6", count_t, (24, 128)), Relay("7", count_d, (24, 128))]
    relays = gains_relays + taps_relays + norm_relays
    count = len(entries)
    shapes = [entry[0].shape[1:] for entry in entries]
    scratch = dict(
        nrm=VM((24, 128), F32),
        gains=VM((8, D), F32),
        shr0=VM((shard, F), F32),
        shr1=VM((shard, F), F32),
        mix=VM((shard, H), F32),
        mer=VM((shard, C), F32),
        gsem=SEMS((8 + dims.ny,)),
        isem=SEMS((count, 3)),
    )
    ins = dict(rates=(rates, SM), kp=(kernel_part, VM))
    outs = dict(norms=((24, 128), F32, VM))
    for i, (params, mean, square, _) in enumerate(entries):
        tag = str(i)
        ins |= {"p" + tag: (params, HB), "m" + tag: (mean, HB), "v" + tag: (square, HB)}
        scratch |= {"w" + tag: VM(shapes[i], F32), "n" + tag: VM(shapes[i], F32)}
        scratch |= {"q" + tag: VM(shapes[i], F32)}
        outs |= {"g" + tag: (shapes[i], F32, VM)}
    for i, part in enumerate(gain_parts):
        ins |= {"d" + str(i): (part, VM)}
    for i, array in enumerate(sums):
        ins |= {"s" + str(i): (array, HB)}
    for relay in relays:
        scratch |= relay.scratch()

    def body(r):
        spot = Spot(dims)
        everyone = [(spot.d, lax.rem(spot.t + j, count_t)) for j in range(1, count_t)]
        items = [(lax.rem(spot.d + j, count_d), spot.t) for j in range(1, count_d)]
        greet(everyone + items)
        get = lambda name, i: getattr(r, name + str(i))
        for k, (i, job) in enumerate(beside.jobs):
            target = r.shr0 if i else r.g0.at[0]
            job.bind(r, spot, get("bi", i), target).start()
        loads = []
        for i in range(count):
            triple = [
                pltpu.make_async_copy(get("p", i).at[0], get("w", i), r.isem.at[i, 0]),
                pltpu.make_async_copy(get("m", i), get("n", i), r.isem.at[i, 1]),
                pltpu.make_async_copy(get("v", i), get("q", i), r.isem.at[i, 2]),
            ]
            for copy in triple:
                copy.start()
            loads.append(triple)
        grads = [
            pltpu.make_async_copy(r.s0, r.g0.at[1], r.gsem.at[0]),
            pltpu.make_async_copy(r.s1, r.shr1, r.gsem.at[1]),
            pltpu.make_async_copy(r.s2.at[:, pl.ds(3 * H, H)], r.mix, r.gsem.at[2]),
            pltpu.make_async_copy(r.s3.at[:, pl.ds(2 * C, C)], r.mer, r.gsem.at[3]),
        ]
        grads += [
            pltpu.make_async_copy(r.s2.at[:, pl.ds(k * H, H)], r.g2.at[k], r.gsem.at[4 + k])
            for k in range(3)
        ]
        sides = [
            pltpu.make_async_copy(r.s3.at[:, pl.ds(k * C, C)], r.g4.at[k], r.gsem.at[7 + k])
            for k in range(2)
        ]
        for copy in grads + sides:
            copy.start()

        r.nrm[...] = jnp.zeros_like(r.nrm)
        row = lax.broadcasted_iota(jnp.int32, (24, 128), 0)
        lane = lax.broadcasted_iota(jnp.int32, (24, 128), 1)
        first_piece = piece_rows(shapes)
        loaded = set()

        def norm(i, p, weight=None):
            if i not in loaded:
                loaded.add(i)
                for copy in loads[i]:
                    copy.wait()
            step = tile_rows(shapes[i])
            columns = shapes[i][-1]
            acc_rows = 8 if step % 8 == 0 else step
            zero = jnp.zeros((acc_rows, columns), F32)

            def tile(j, carry):
                rs = pl.ds(pl.multiple_of(j * step, step), step)
                master = get("w", i)[p, rs, :]
                mean, square = moments_of(
                    get("g", i)[p, rs, :], get("n", i)[p, rs, :], get("q", i)[p, rs, :], r.rates
                )
                step_of = direction_of(mean, square, master, r.rates, entries[i][3])
                return (
                    carry[0] + eighths(master * master),
                    carry[1] + eighths(step_of * step_of),
                )

            totals = lax.fori_loop(0, shapes[i][-2] // step, tile, (zero, zero))
            here = row == first_piece[i] + p
            for column, total in enumerate(totals):
                value = jnp.sum(jnp.sum(total, axis=0, keepdims=True), axis=1, keepdims=True)
                if weight is not None:
                    value = value * weight
                r.nrm[...] += jnp.where(jnp.logical_and(here, lane == column), value, 0.0)

        r.gains[...] = jnp.zeros_like(r.gains)
        for k in range(5):
            r.gains[k : k + 1, :] = jnp.sum(get("d", k)[...], axis=0, keepdims=True)
        gains_relays[0].start(r, spot.c, [spot.sibling()], r.gains[...])
        slow = [spot.slow(j) for j in range(1, dims.na)]
        fast = [spot.fast(j) for j in range(1, dims.nb)]
        taps_relays[0].start(r, spot.a, slow, r.kp[...])
        total = gains_relays[0].finish()
        gains_relays[1].start(r, spot.y, [spot.across(j) for j in range(1, dims.ny)], total)
        for copy in grads + sides:
            copy.wait()
        flip(r.g3.at[0], r.mix, dims)
        flip(r.g5.at[0], r.mer, dims)
        total = gains_relays[1].finish()
        gains_relays[2].start(r, spot.a, slow, total)
        for i in (2, 3, 4, 5):
            for p in range(shapes[i][0]):
                norm(i, p)
        jobs = [job for _, job in beside.jobs]
        half = len(jobs) // 2
        jobs[0].advance()
        norm(0, 1)
        for job in jobs[1:half]:
            job.advance()
        flip(r.g1.at[1], r.shr1, dims)
        norm(1, 1)
        total = taps_relays[0].finish()
        taps_relays[1].start(r, spot.b, fast, total)
        total = gains_relays[2].finish()
        gains_relays[3].start(r, spot.b, fast, total)
        for job in jobs[half:]:
            job.advance()
        r.g6[0] = taps_relays[1].finish()
        owner = jnp.where(spot.d == 0, 1.0, 0.0)
        norm(6, 0, owner)
        r.gains[...] = gains_relays[3].finish()
        owner = jnp.where(spot.t == 0, owner, 0.0)
        for k in range(5):
            r.g7[k] = r.gains[k : k + 1, :]
            norm(7, k, owner)
        for job in jobs[:half]:
            job.finish()
        norm(0, 0)
        for job in jobs[half:]:
            job.finish()
        flip(r.g1.at[0], r.shr0, dims)
        norm(1, 0)
        norm_relays[0].start(r, spot.t, everyone, r.nrm[...])
        total = norm_relays[0].finish()
        norm_relays[1].start(r, spot.d, items, total)
        r.norms[...] = norm_relays[1].finish()

    return call(body, ins | beside.ins(), outs, scratch | beside.scratch(), cid)


def update_kernel(dims, rates, norms, entries, grads):
    count = len(entries)
    shapes = [entry[1].shape for entry in entries]
    ins = dict(rates=(rates, SM), norms=(norms, VM))
    outs = dict(trust=((17, 2), F32, VM))
    scratch = dict(isem=SEMS((count, 5)), osem=SEMS((count, 5)))
    for i, (params, mean, square, _) in enumerate(entries):
        tag = str(i)
        shape = shapes[i]
        pair = (2,) + shape
        ins |= {"p" + tag: (params, HB), "m" + tag: (mean, HB), "v" + tag: (square, HB)}
        ins |= {"g" + tag: (grads[i], HB)}
        scratch |= {"w" + tag: VM(pair, F32), "n" + tag: VM(shape, F32)}
        scratch |= {"q" + tag: VM(shape, F32), "h" + tag: VM(shape, F32)}
        scratch |= {"b" + tag: VM(pair, BF16)}
        outs |= {"og" + tag: (shape, F32, HB), "om" + tag: (shape, F32, HB)}
        outs |= {"ov" + tag: (shape, F32, HB), "ow" + tag: (pair, F32, HB)}
        outs |= {"ob" + tag: (pair, BF16, HB)}
    order = [7, 6] + list(range(2, 6)) + [0, 1]

    def body(r):
        get = lambda name, i: getattr(r, name + str(i))
        loads, stores = {}, []
        for i in order:
            moves = (("g", "h"), ("m", "n"), ("v", "q"), ("p", "w"))
            loads[i] = [
                pltpu.make_async_copy(get(source, i), get(target, i), r.isem.at[i, k])
                for k, (source, target) in enumerate(moves)
            ]
            for copy in loads[i]:
                copy.start()
        norms = jnp.sqrt(r.norms[...])
        r.trust[...] = norms[:17, :2]
        ratio = r.rates[3] * norms[:, 0:1] / norms[:, 1:2]

        def send(i, name, target, k):
            copy = pltpu.make_async_copy(get(name, i), get(target, i), r.osem.at[i, k])
            copy.start()
            stores.append(copy)

        for i in order:
            for copy in loads[i]:
                copy.wait()
            send(i, "h", "og", 0)
            step = tile_rows(shapes[i])
            offset = piece_rows(shapes)[i]
            for p in range(shapes[i][0]):
                scale = ratio[offset + p : offset + p + 1, :]

                def tile(j, p=p, i=i, step=step, scale=scale):
                    rs = pl.ds(pl.multiple_of(j * step, step), step)
                    master = get("w", i)[0, p, rs, :]
                    mean, square = moments_of(
                        get("h", i)[p, rs, :], get("n", i)[p, rs, :], get("q", i)[p, rs, :], r.rates
                    )
                    move = direction_of(mean, square, master, r.rates, entries[i][3])
                    master = master - scale * move
                    average = get("w", i)[1, p, rs, :]
                    average = r.rates[2] * average + (1.0 - r.rates[2]) * master
                    get("n", i)[p, rs, :] = mean
                    get("q", i)[p, rs, :] = square
                    get("w", i)[0, p, rs, :] = master
                    get("w", i)[1, p, rs, :] = average
                    get("b", i)[0, p, rs, :] = master.astype(BF16)
                    get("b", i)[1, p, rs, :] = average.astype(BF16)

                loop(shapes[i][-2] // step, tile)
            send(i, "n", "om", 1)
            send(i, "q", "ov", 2)
            send(i, "w", "ow", 3)
            send(i, "b", "ob", 4)
        for copy in stores:
            copy.wait()

    return call(body, ins, outs, scratch, None)


def product(operand, another):
    return jnp.dot(operand, another, preferred_element_type=F32)


def product_left(operand, another):
    return lax.dot_general(
        operand, another, (((0,), (0,)), ((), ())), preferred_element_type=F32
    )


def product_right(operand, another):
    return lax.dot_general(
        operand, another, (((1,), (1,)), ((), ())), preferred_element_type=F32
    )


def silu_slope(before):
    sigmoid_of = jax.nn.sigmoid(before)
    return sigmoid_of * (1.0 + before * (1.0 - sigmoid_of))


def attend(queries, keys_all, values_all, live_keys):
    score_scale = HEAD_DIM ** (-0.5)
    slot, heads_local = queries.shape[:2]
    blocks = queries.reshape(slot // BLOCK, BLOCK, heads_local, HEAD_DIM)

    def one_block(query_block):
        scores = (
            jnp.einsum("bhe,khe->hbk", query_block, keys_all, preferred_element_type=F32)
            * score_scale
        )
        scores = jnp.where(live_keys[None, None, :], scores, MASKED)
        row_peak = jnp.max(scores, axis=-1, keepdims=True)
        exponent = jnp.exp(scores - row_peak)
        row_total = jnp.sum(exponent, axis=-1, keepdims=True)
        weights = (exponent / row_total).astype(BF16)
        output = jnp.einsum("hbk,khe->bhe", weights, values_all, preferred_element_type=F32)
        return (output, (row_peak + jnp.log(row_total))[..., 0])

    outputs, logsum = lax.map(one_block, blocks)
    return (outputs.reshape(slot, heads_local, HEAD_DIM), logsum)


def attend_back(queries, keys_all, values_all, live_keys, logsum, grad_out):
    score_scale = HEAD_DIM ** (-0.5)
    slot, heads_local = queries.shape[:2]
    blocks = queries.reshape(slot // BLOCK, BLOCK, heads_local, HEAD_DIM)
    grad_blocks = grad_out.reshape(slot // BLOCK, BLOCK, heads_local, HEAD_DIM)

    def one_block(carried, inputs):
        key_grad, value_grad = carried
        query_block, grad_block, logsum_block = inputs
        scores = (
            jnp.einsum("bhe,khe->hbk", query_block, keys_all, preferred_element_type=F32)
            * score_scale
        )
        scores = jnp.where(live_keys[None, None, :], scores, MASKED)
        probability = jnp.exp(scores - logsum_block[..., None])
        weights = probability.astype(BF16)
        value_grad = value_grad + jnp.einsum(
            "hbk,bhe->khe", weights, grad_block, preferred_element_type=F32
        )
        prob_grad = jnp.einsum(
            "bhe,khe->hbk", grad_block, values_all, preferred_element_type=F32
        )
        row_inner = jnp.sum(probability * prob_grad, axis=-1, keepdims=True)
        score_grad = (probability * (prob_grad - row_inner)).astype(BF16)
        query_grad = (
            jnp.einsum("hbk,khe->bhe", score_grad, keys_all, preferred_element_type=F32)
            * score_scale
        )
        key_grad = (
            key_grad
            + jnp.einsum("hbk,bhe->khe", score_grad, query_block, preferred_element_type=F32)
            * score_scale
        )
        return ((key_grad, value_grad), query_grad)

    zeroed = jnp.zeros((slot, heads_local, HEAD_DIM), F32)
    (key_grad, value_grad), query_grad = lax.scan(
        one_block, (zeroed, zeroed), (blocks, grad_blocks, logsum)
    )
    return (query_grad.reshape(slot, heads_local, HEAD_DIM), key_grad, value_grad)


def attention_forward(dims, normed, matrices, live_keys):
    S, H = dims.S, dims.H
    packed = product(normed, matrices[:, : 3 * H]).astype(BF16)
    queries, keys_all, values_all = (
        packed[:, i * H : (i + 1) * H].reshape(S, H // HEAD_DIM, HEAD_DIM) for i in range(3)
    )
    output, logsum = attend(queries, keys_all, values_all, live_keys)
    mixed_heads = output.reshape(S, H).astype(BF16)
    part = product_right(mixed_heads, matrices[:, 3 * H :])
    return part, (queries, keys_all, values_all, mixed_heads, logsum)


def attention_back(dims, normed, matrices, live_keys, kept, upstream):
    S, H = dims.S, dims.H
    queries, keys_all, values_all, mixed_heads, logsum = kept
    mixing_grad = product_left(upstream, mixed_heads)
    mixed_grad = product(upstream, matrices[:, 3 * H :]).astype(BF16)
    grads = attend_back(
        queries,
        keys_all,
        values_all,
        live_keys,
        logsum,
        mixed_grad.reshape(S, H // HEAD_DIM, HEAD_DIM),
    )
    packed_grad = jnp.concatenate([grad.reshape(S, H).astype(BF16) for grad in grads], axis=1)
    project_grad = product_left(normed, packed_grad)
    part = product_right(packed_grad, matrices[:, : 3 * H])
    return part, jnp.concatenate([project_grad, mixing_grad], axis=1).astype(BF16)


def conv_forward(dims, normed, matrices, taps, live):
    S, C = dims.S, dims.C
    pair = product(normed, matrices[:, : 2 * C])
    values, gate = pair[:, :C], jax.nn.sigmoid(pair[:, C:])
    glu_values = values * gate * live
    margin = (KERNEL - 1) // 2
    padded = jnp.pad(glu_values, ((margin, margin), (0, 0)))
    mixed_time = padded[0:S] * taps[0]
    for offset in range(1, KERNEL):
        mixed_time = mixed_time + padded[offset : offset + S] * taps[offset]
    hidden = jax.nn.silu(mixed_time).astype(BF16)
    part = product_right(hidden, matrices[:, 2 * C :])
    return part, (values, gate, padded, mixed_time, hidden)


def conv_back(dims, normed, matrices, taps, live, kept, upstream):
    S, C = dims.S, dims.C
    values, gate, padded, mixed_time, hidden = kept
    merging_grad = product_left(upstream, hidden)
    time_grad = product(upstream, matrices[:, 2 * C :]) * silu_slope(mixed_time)
    margin = (KERNEL - 1) // 2
    kernel_grad = jnp.stack(
        [jnp.sum(padded[offset : offset + S] * time_grad, axis=0) for offset in range(KERNEL)]
    )
    slope_padded = jnp.pad(time_grad, ((margin, margin), (0, 0)))
    glu_grad = slope_padded[2 * margin : 2 * margin + S] * taps[0]
    for offset in range(1, KERNEL):
        first = 2 * margin - offset
        glu_grad = glu_grad + slope_padded[first : first + S] * taps[offset]
    glu_grad = glu_grad * live
    pair_grad = jnp.concatenate(
        [glu_grad * gate, glu_grad * values * gate * (1.0 - gate)], axis=1
    ).astype(BF16)
    gating_grad = product_left(normed, pair_grad)
    part = product_right(pair_grad, matrices[:, : 2 * C])
    return part, jnp.concatenate([gating_grad, merging_grad], axis=1).astype(BF16), kernel_grad


def shards(
    dims,
    frames_input,
    out_grad,
    lengths,
    step_count,
    rates,
    expand_params,
    expand_first,
    expand_second,
    shrink_params,
    shrink_first,
    shrink_second,
    project_params,
    project_first,
    project_second,
    mixing_params,
    mixing_first,
    mixing_second,
    gating_params,
    gating_first,
    gating_second,
    kernel_params,
    kernel_first,
    kernel_second,
    merging_params,
    merging_first,
    merging_second,
    gains_params,
    gains_first,
    gains_second,
):
    local_rows, width = frames_input.shape
    shard_rows = expand_params.shape[2]
    dims = SimpleNamespace(
        L=local_rows,
        D=width,
        S=local_rows * dims.ny * 2,
        F=expand_params.shape[3],
        H=project_params.shape[3],
        C=gating_params.shape[3],
        **vars(dims),
    )
    tensor_rank = lax.axis_index("tensor")
    data_rank = lax.axis_index("dp")
    block_y = tensor_rank // 2
    live_keys = jnp.arange(dims.S, dtype=jnp.int32) < lengths[0]
    live = live_keys.astype(F32).reshape(-1, 1)
    live_local = lax.dynamic_slice_in_dim(live, tensor_rank * local_rows, local_rows, 0)
    taps = kernel_params[0]
    gain = [gains_params[0, i : i + 1] for i in range(5)]

    expand_shard = expand_params[0].astype(BF16)
    shrink_shard = jnp.swapaxes(shrink_params[0].astype(BF16), 1, 2)
    attention_shard = jnp.concatenate(
        [project_params[0, 0], project_params[0, 1], project_params[0, 2], mixing_params[0].T], axis=1
    ).astype(BF16)
    conv_shard = jnp.concatenate(
        [gating_params[0, 0], gating_params[0, 1], merging_params[0].T], axis=1
    ).astype(BF16)
    cotangent = (out_grad.astype(F32) * live_local).astype(BF16)

    head = head_kernel(
        dims, 0, frames_input, cotangent, gain[0], expand_shard[0], shrink_shard[0]
    )
    n1, h0, expand0, shrink0 = head["n"], head["xh"], head["bo0"], head["bo1"]
    one = ff_forward(
        dims, 1, n1, expand0, shrink0, h0, gain[1], Beside(dims, [attention_shard, conv_shard])
    )
    n2, h1 = one["nn"], one["hn"]
    attention_matrices, conv_matrices = one["bo0"], one["bo1"]
    part, kept_two = attention_forward(dims, n2, attention_matrices, live_keys)
    two = edge_forward(
        dims, 2, part, h1, gain[2], Beside(dims, [expand_shard[1]])
    )
    n3, h2, expand1 = two["nn"], two["hn"], two["bo0"]
    part, kept_three = conv_forward(dims, n3, conv_matrices, taps, live)
    three = edge_forward(dims, 3, part, h2, gain[3], Beside(dims, [shrink_shard[1]]))
    n4, h3, shrink1 = three["nn"], three["hn"], three["bo0"]
    four = ff_turn(
        dims, 4, n4, expand1, shrink1, h3, gain[4], head["ogh"], Beside(dims)
    )
    five = ff_back(
        dims, 5, four["w"], expand1, shrink1, four["slope"], four["u"], n4, four["ghn"], h3,
        gain[3], Beside(dims), False,
    )
    def blocks(array):
        return array.reshape(dims.na, dims.nb, shard_rows, array.shape[1])

    part, conv_grad, kernel_grad = conv_back(
        dims, n3, conv_matrices, taps, live, kept_three, five["wn"]
    )
    six = edge_back(
        dims, 6, part, five["ghn"], h2, gain[2], 1.0,
        Beside(dims, scatters=[blocks(conv_grad), blocks(five["dr"])]),
    )
    part, attention_grad = attention_back(
        dims, n2, attention_matrices, live_keys, kept_two, six["wn"]
    )
    seven = edge_back(
        dims, 7, part, six["ghn"], h1, gain[1], 0.5, Beside(dims, scatters=[blocks(five["de"])])
    )
    eight = ff_back(
        dims, 8, seven["wn"], expand0, shrink0, one["slope"], one["u"], n1, seven["ghn"], h0,
        gain[0], Beside(dims, scatters=[blocks(attention_grad)]), True,
    )
    frames_out = lax.dynamic_index_in_dim(four["fo"], block_y, 0, False)

    steps_done = step_count[0].astype(F32)
    scalars = jnp.concatenate(
        [rates, 1.0 / (1.0 - rates[:2] ** steps_done), jnp.zeros((2,), F32)]
    )
    entries = []
    triples = (
        (expand_params, expand_first, expand_second),
        (shrink_params, shrink_first, shrink_second),
        (project_params, project_first, project_second),
        (mixing_params, mixing_first, mixing_second),
        (gating_params, gating_first, gating_second),
        (kernel_params, kernel_first, kernel_second),
        (merging_params, merging_first, merging_second),
        (gains_params, gains_first, gains_second),
    )
    for place in PLACES:
        params, first, second = triples[place]
        if first.ndim == 2:
            at = 1 if place == 7 else 0
            params = jnp.expand_dims(params, at + 1)
            first, second = jnp.expand_dims(first, at), jnp.expand_dims(second, at)
        entries.append((params, first, second, 0.0 if place == 7 else DECAY_RATE))
    summed = gradient_kernel(
        dims, 9, scalars, entries, [blocks(eight["de"]), blocks(eight["dr"])],
        [seven["bo0"], six["bo1"], eight["bo0"], six["bo0"]],
        [kernel["dg"] for kernel in (eight, seven, six, five, four)], kernel_grad,
    )
    updated = update_kernel(
        dims, scalars, summed["norms"], entries, [summed["g" + str(i)] for i in range(8)]
    )
    results = []
    for place in range(8):
        tag = str(PLACES.index(place))
        like = triples[place][1].shape
        results += [updated[name + tag].reshape(like) for name in ("og", "om", "ov")]
        results += [updated[name + tag].reshape((2,) + like) for name in ("ow", "ob")]
    return (frames_out, eight["gin"], *results, updated["trust"])


def solution(mesh):
    slow = math.gcd(mesh.shape["dp"], 4)
    dims = SimpleNamespace(na=slow, nb=mesh.shape["dp"] // slow, ny=mesh.shape["tensor"] // 2)
    return jax.shard_map(
        functools.partial(shards, dims),
        mesh=mesh,
        in_specs=(
            P(("dp", "tensor"), None),
            P(("dp", "tensor"), None),
            P("dp"),
            P(),
            P(),
            P(None, None, "dp", "tensor"),
            P(None, "dp", "tensor"),
            P(None, "dp", "tensor"),
            P(None, None, "tensor", "dp"),
            P(None, "tensor", "dp"),
            P(None, "tensor", "dp"),
            P(None, None, "dp", "tensor"),
            P(None, "dp", "tensor"),
            P(None, "dp", "tensor"),
            P(None, "tensor", "dp"),
            P("tensor", "dp"),
            P("tensor", "dp"),
            P(None, None, "dp", "tensor"),
            P(None, "dp", "tensor"),
            P(None, "dp", "tensor"),
            P(None, None, "tensor"),
            P(None, "tensor"),
            P(None, "tensor"),
            P(None, "tensor", "dp"),
            P("tensor", "dp"),
            P("tensor", "dp"),
            P(),
            P(),
            P(),
        ),
        out_specs=(
            P(("dp", "tensor"), None),
            P(("dp", "tensor"), None),
            P(None, "dp", "tensor"),
            P(None, "dp", "tensor"),
            P(None, "dp", "tensor"),
            P(None, None, "dp", "tensor"),
            P(None, None, "dp", "tensor"),
            P(None, "tensor", "dp"),
            P(None, "tensor", "dp"),
            P(None, "tensor", "dp"),
            P(None, None, "tensor", "dp"),
            P(None, None, "tensor", "dp"),
            P(None, "dp", "tensor"),
            P(None, "dp", "tensor"),
            P(None, "dp", "tensor"),
            P(None, None, "dp", "tensor"),
            P(None, None, "dp", "tensor"),
            P("tensor", "dp"),
            P("tensor", "dp"),
            P("tensor", "dp"),
            P(None, "tensor", "dp"),
            P(None, "tensor", "dp"),
            P(None, "dp", "tensor"),
            P(None, "dp", "tensor"),
            P(None, "dp", "tensor"),
            P(None, None, "dp", "tensor"),
            P(None, None, "dp", "tensor"),
            P(None, "tensor"),
            P(None, "tensor"),
            P(None, "tensor"),
            P(None, None, "tensor"),
            P(None, None, "tensor"),
            P("tensor", "dp"),
            P("tensor", "dp"),
            P("tensor", "dp"),
            P(None, "tensor", "dp"),
            P(None, "tensor", "dp"),
            P(),
            P(),
            P(),
            P(),
            P(),
            P(),
        ),
        check_vma=False,
    )
```

time: 1640 us -> 691 us (0.42)
  waiting for transfers between devices: 1130 us -> 0 us
  Pallas kernels: 0 us -> 523 us
  blocking collectives: 150 us -> 0 us
  other arithmetic: 135 us -> 36.4 us
  matrix products: 135 us -> 77.6 us
  between operations: 25.6 us -> 3.4 us
  local copies, waits for them, and re-layouts: 59.2 us -> 41 us
    reduce_scatter x14 -> x0, waiting for transfers between devices: 789 us -> none  [the longest x4 171 us: leave_rows(): lax.psum_scatter(partial_sum, 'tensor', scatter_dimension=0, tiled=True)]
    pallas_call x0 -> x11, Pallas kernels: none -> 523 us  [call(): pl.pallas_call(kernel, out_shape=[jax.ShapeDtypeStruct(shape, kind) for s...]
    all_gather x12 -> x0, waiting for transfers between devices: 339 us -> none  [the longest x4 90.2 us: enter_rows(): lax.all_gather(normed.astype(jnp.bfloat16), 'tensor', axis=0, tiled=True)]
    psum x3 -> x0, blocking collectives: 90.1 us -> none  [the longest x1 39.7 us: shards(): gains_sum, kernel_sum = lax.psum((gains_grad, kernel_grad), 'dp')]
    reduce_sum x32 -> x1, other arithmetic: 65.4 us -> 2.85 us  [conv_back(): jnp.sum(padded[offset:offset + S] * time_grad, axis=0)]
    all_gather x2 -> x0, blocking collectives: 59.5 us -> none  [the longest x1 30 us: shards(): lax.all_gather(mixing_params[0].astype(jnp.bfloat16), 'dp', axis=1, tiled...]
    dot_general x18 -> x10, matrix products: 66.6 us -> 38.4 us  [the longest x4 16 us: product(): return jnp.dot(operand, another, preferred_element_type=F32)]
    dot_general x6 -> x4, matrix products: 35.8 us -> 13.6 us  [product_right(): lax.dot_general(operand, another, (((1,), (1,)), ((), ())), preferred_ele...]
  transfers between devices with their start and end apart: 26 -> 0, of which waited for: 26 -> 0; matrix products, arithmetic and copies ran while one was open for 8% -> 0% of each run, Pallas kernels for 0% -> 0%
where the time goes in v1:
time: 691 us; the launch traced here: 682 us
  Pallas kernels  523 us (76%)
  matrix products  77.6 us (11%)
  local copies, waits for them, and re-layouts  41 us (6%)
  other arithmetic  36.4 us (5%)
    pallas_call x11, Pallas kernels, call(): pl.pallas_call(kernel, out_shape=[jax.ShapeDtypeStruct(shape, kind) for s...  523 us
    unnamed x120, local copies, waits for them, and re-layouts  20.3 us
    dot_general x4, matrix products, product(): return jnp.dot(operand, another, preferred_element_type=F32)  16 us

profile of v1, /device:TPU:0, one launch (start us, length us, event | category | flops | bytes accessed | tf_op | source)
XLA Modules:
  0.0 682.2 jit_solution(4049468347488734446)
XLA Ops:
  7.9 61.9 %shard_map.612 = (bf16[2,256,1024]{2,1,0:T(8,128)(2,1)S(1)}, bf16[2,256,1024]{2,1,0:T(8,128)(2,1)S(1)}, bf16[1024,1024]{1,0:T(8,128)(2,1)}, bf16[1024,1024]{1,0:T(8,128)(2,1)}, bf16[1024,1024]{1,0:T(8,128)(2,1)}) custom-call(bf16[256,1024]{1,0:T(8,128)(2,1)S(1)} %copy-done.14, bf16[256,1024]{1,0:T(8,128)(2,1)S(1)} %multiply_convert_fusion.4.refs_1_, ...), custom_call_target="tpu_custom_call" | custom-call | tf_op jit(solution)/shard_map/pallas_call | solution.py:97
  73.7 52.1 %shard_map.613 = (bf16[1024,1024]{1,0:T(8,128)(2,1)}, bf16[1024,1024]{1,0:T(8,128)(2,1)}, f32[2,256,1024]{2,1,0:T(8,128)}, bf16[1024,1024]{1,0:T(8,128)(2,1)}, b...) custom-call(bf16[1024,1024]{1,0:T(8,128)(2,1)} %get-tuple-element.227.refs_0_.refs_5_, ...), custom_call_target="tpu_custom_call" | custom-call | tf_op jit(solution)/shard_map/pallas_call | solution.py:97
  125.9 4.4 convolution_convert_fusion.1
  136.4 16.5 %while.28 = (s32[]{:T(128)}, bf16[2,512,4,64]{1,3,2,0:T(8,128)(2,1)}, f32[2,4,512]{2,1,0:T(4,128)S(1)}, bf16[2,512,4,64]{1,3,2,0:T(8,128)(2,1)}, bf16[1024,4,64]...) while((s32[]{:T(128)}, bf16[2,512,4,64]{1,3,2,0:T(8,128)(2,1)}, ...), condition=%wide.region_3.4_spmd.clone, body=%wide.region_0.3_spmd.clone.sunk | while | flops 562035712 | bytes 29168760 | solution.py:1280
  141.5 3.1 fusion.129
  149.7 3.1 fusion.129
  154.5 3.9 fusion.81.refs_0_
  158.5 42.9 %shard_map.614 = (f32[2,256,1024]{2,1,0:T(8,128)S(1)}, bf16[1024,1024]{1,0:T(8,128)(2,1)}, bf16[1024,1024]{1,0:T(8,128)(2,1)}) custom-call(f32[1024,1024]{1,0:T(8,128)} %fusion.81.refs_0_, f32[2,256,1024]{2,1,0:T(8,128)} %get-tuple-element.234.refs_1_.refs_2_, f32[1,1024]{1,0:T(1,128)S(1)} %get-tuple-element.613.refs_2_.refs_3_, ...), custom_call_target="tpu_custom_call" | custom-call | tf_op jit(solution)/shard_map/pallas_call | solution.py:97
  201.3 3.6 fusion.74
  205.9 4.1 multiply_add_fusion
  212.7 42.1 %shard_map.615 = (f32[2,256,1024]{2,1,0:T(8,128)S(1)}, bf16[1024,1024]{1,0:T(8,128)(2,1)}, bf16[1024,1024]{1,0:T(8,128)(2,1)}) custom-call(f32[1024,1024]{1,0:T(8,128)} %fusion.78.refs_0_, f32[2,256,1024]{2,1,0:T(8,128)} %copy-done.1, f32[1,1024]{1,0:T(1,128)S(1)} %get-tuple-element.612.refs_2_.refs_8_, bf16[128,1024]{1,0:T(8,128)(2,1)S(1)} %get-tuple-element.573.refs_3_), custom_call_target="tpu_custom_call" | custom-call | tf_op jit(solution)/shard_map/pallas_call | solution.py:97
  256.1 42.1 %shard_map.616 = (bf16[1024,1024]{1,0:T(8,128)(2,1)}, bf16[1024,1024]{1,0:T(8,128)(2,1)}, bf16[2,256,1024]{2,1,0:T(8,128)(2,1)S(1)}, f32[2,256,1024]{2,1,0:T(8,1...) custom-call(bf16[1024,1024]{1,0:T(8,128)(2,1)} %get-tuple-element.238.refs_0_.refs_5_, ...), custom_call_target="tpu_custom_call" | custom-call | tf_op jit(solution)/shard_map/pallas_call | solution.py:97
  299.2 43.8 %shard_map.617 = (f32[2,256,1024]{2,1,0:T(8,128)S(1)}, bf16[1024,1024]{1,0:T(8,128)(2,1)}, bf16[1024,1024]{1,0:T(8,128)(2,1)}, bf16[1024,1024]{1,0:T(8,128)(2,1)}, f32[8,1024]{1,0:T(8,128)S(1)}) custom-call(bf16[1024,1024]{1,0:T(8,128)(2,1)} %get-tuple-element.245.refs_0_, bf16[1024,1024]{1,0:T(8,128)(2,1)} %get-tuple-element.239.refs_1_, ...), custom_call_target="tpu_custom_call" | custom-call | tf_op jit(solution)/shard_map/pallas_call | solution.py:97
  343.0 4.8 multiply_reduce_fusion.19
  350.8 6.4 multiply_convert_fusion.2
  363.0 3.2 fusion.72.refs_0_
  366.2 59.0 %shard_map.618 = (f32[2,256,1024]{2,1,0:T(8,128)}, bf16[1024,1024]{1,0:T(8,128)(2,1)}, f32[8,1024]{1,0:T(8,128)S(1)}, f32[128,768]{1,0:T(8,128)S(1)}, f32[128,1024]{1,0:T(8,128)S(1)}) custom-call(f32[1024,1024]{1,0:T(8,128)} %fusion.72.refs_0_, f32[2,256,1024]{2,1,0:T(8,128)} %copy-done.3, f32[2,256,1024]{2,1,0:T(8,128)} %copy-done.1, ...), custom_call_target="tpu_custom_call" | custom-call | tf_op jit(solution)/shard_map/pallas_call | solution.py:97
  426.8 3.2 convolution_convert_fusion.4
  434.3 39.7 %while.29 = (s32[]{:T(128)}, f32[1024,4,64]{0,2,1:T(8,128)S(1)}, f32[1024,4,64]{0,2,1:T(8,128)}, bf16[2,512,4,64]{1,3,2,0:T(8,128)(2,1)}, bf16[2,512,4,64]{1,3,2...) while((s32[]{:T(128)}, f32[1024,4,64]{0,2,1:T(8,128)S(1)}, ...), condition=%wide.region_6.7_spmd.clone, body=%wide.region_4.6_spmd.clone.sunk | while | flops 1375075328 | bytes 143848336 | solution.py:1320
  439.3 3.5 multiply_convert_fusion.8
  442.8 3.3 fusion.140
  446.2 4.6 fusion.142
  458.5 3.5 multiply_convert_fusion.8
  462.0 3.3 fusion.140
  465.4 4.6 fusion.142
  470.0 3.9 fusion.141
  479.7 4.2 copy.108
  489.2 3.8 fusion.45.refs_0_
  492.9 42.8 %shard_map.619 = (f32[2,256,1024]{2,1,0:T(8,128)S(1)}, bf16[1024,1024]{1,0:T(8,128)(2,1)}, f32[8,1024]{1,0:T(8,128)S(1)}, f32[128,1024]{1,0:T(8,128)S(1)}) custom-call(f32[1024,1024]{1,0:T(8,128)} %fusion.45.refs_0_, f32[2,256,1024]{2,1,0:T(8,128)} %get-tuple-element.256.refs_1_, f32[2,256,1024]{2,1,0:T(8,128)} %get-tuple-element.234.refs_1_.refs_2_, ...), custom_call_target="tpu_custom_call" | custom-call | tf_op jit(solution)/shard_map/pallas_call | solution.py:97
  537.2 50.7 %shard_map.620 = (bf16[256,1024]{1,0:T(8,128)(2,1)S(1)}, bf16[1024,1024]{1,0:T(8,128)(2,1)}, bf16[1024,1024]{1,0:T(8,128)(2,1)}, f32[8,1024]{1,0:T(8,128)S(1)}, f32[128,1024]{1,0:T(8,128)S(1)}) custom-call(bf16[1024,1024]{1,0:T(8,128)(2,1)} %get-tuple-element.258.refs_0_, bf16[1024,1024]{1,0:T(8,128)(2,1)} %get-tuple-element.228.refs_1_, ...), custom_call_target="tpu_custom_call" | custom-call | tf_op jit(solution)/shard_map/pallas_call | solution.py:97
  589.8 72.3 %shard_map.621 = (f32[24,128]{1,0:T(8,128)S(1)}, f32[2,128,1024]{2,1,0:T(8,128)}, f32[2,1024,128]{2,1,0:T(8,128)}, f32[3,128,256]{2,1,0:T(8,128)S(1)}, f32[1,256...) custom-call(f32[8]{0:T(128)S(1)} %pad_maximum_fusion.10.refs_0_, ...), custom_call_target="tpu_custom_call" | custom-call | tf_op jit(solution)/shard_map/pallas_call | solution.py:97
  662.1 13.5 %shard_map.622 = (f32[17,2]{1,0:T(8,128)S(1)}, f32[2,128,1024]{2,1,0:T(8,128)}, f32[2,128,1024]{2,1,0:T(8,128)}, f32[2,128,1024]{2,1,0:T(8,128)}, f32[2,2,128,10...) custom-call(f32[8]{0:T(128)S(1)} %pad_maximum_fusion.10.refs_0_, ...), custom_call_target="tpu_custom_call" | custom-call | tf_op jit(solution)/shard_map/pallas_call | solution.py:97
  (223 shorter events, 80.2 us)
Async XLA Ops:
  1.4 203.6 %copy-start.54 = (f32[1024]{0:T(1024)}, f32[1024]{0:T(1024)S(1)}, u32[]{:S(2)}) copy-start(f32[1024]{0:T(1024)S(1)} %fusion.83) | copy-start | bytes 12292
  6.8 63.1 %copy-start.33 = (f32[2,3,128,256]{3,2,1,0:T(8,128)S(1)}, f32[2,3,128,256]{3,2,1,0:T(8,128)}, u32[]{:S(2)}) copy-start(f32[2,3,128,256]{3,2,1,0:T(8,128)} %refs_10_.3) | copy-start | bytes 2359300
  152.8 5.6 copy-start.51
  158.4 42.9 %copy-start.24 = (bf16[1024,768]{1,0:T(8,128)(2,1)S(1)}, bf16[1024,768]{1,0:T(8,128)(2,1)}, u32[]{:S(2)}) copy-start(bf16[1024,768]{1,0:T(8,128)(2,1)} %copy-done.23) | copy-start | bytes 4718596
  205.0 5.1 copy-start.31
  210.0 133.0 %copy-start.40 = (f32[1024,256]{1,0:T(8,128)}, f32[1024,256]{1,0:T(8,128)S(1)}, u32[]{:S(2)}) copy-start(f32[1024,256]{1,0:T(8,128)S(1)} %multiply_add_fusion) | copy-start | bytes 3145732
  343.0 4.8 copy-start.3
  350.8 6.4 copy-start.32
  442.8 8.0 %copy-start.27 = (f32[4,512,1024]{2,1,0:T(8,128)S(1)}, f32[4,512,1024]{2,1,0:T(8,128)}, u32[]{:S(2)}) copy-start(f32[4,512,1024]{2,1,0:T(8,128)} %copy-done.26) | copy-start | bytes 25165828 | tf_op jit(solution)/shard_map/while
  446.1 4.7 copy-start.35
  446.1 4.6 copy-start.39
  462.0 8.0 %copy-start.27 = (f32[4,512,1024]{2,1,0:T(8,128)S(1)}, f32[4,512,1024]{2,1,0:T(8,128)}, u32[]{:S(2)}) copy-start(f32[4,512,1024]{2,1,0:T(8,128)} %copy-done.26) | copy-start | bytes 25165828 | tf_op jit(solution)/shard_map/while
  465.3 4.7 copy-start.35
  465.4 4.6 copy-start.39
  537.1 50.9 %copy-start.16 = (f32[128,1024]{1,0:T(8,128)}, f32[128,1024]{1,0:T(8,128)S(1)}, u32[]{:S(2)}) copy-start(f32[128,1024]{1,0:T(8,128)S(1)} %get-tuple-element.268.refs_31_) | copy-start | bytes 1572868
  537.1 51.7 %copy-start.49 = (f32[2,31,256]{2,0,1:T(2,128)S(1)}, f32[2,31,256]{2,0,1:T(2,128)}, u32[]{:S(2)}) copy-start(f32[2,31,256]{2,0,1:T(2,128)} %param.53) | copy-start | bytes 190468
  537.1 51.7 %copy-start.53 = (f32[2,5,1024]{2,0,1:T(2,128)S(1)}, f32[2,5,1024]{2,0,1:T(2,128)}, u32[]{:S(2)}) copy-start(f32[2,5,1024]{2,0,1:T(2,128)} %param.59) | copy-start | bytes 122884
  537.1 51.8 %copy-start.56 = (f32[5,1024]{1,0:T(8,128)S(1)}, f32[5,1024]{1,0:T(8,128)}, u32[]{:S(2)}) copy-start(f32[5,1024]{1,0:T(8,128)} %param.60) | copy-start | bytes 61444
  537.1 51.8 %copy-start.57 = (f32[5,1024]{1,0:T(8,128)S(1)}, f32[5,1024]{1,0:T(8,128)}, u32[]{:S(2)}) copy-start(f32[5,1024]{1,0:T(8,128)} %param.61) | copy-start | bytes 61444
  537.1 52.5 %copy-start.58 = (f32[4]{0:T(128)S(1)}, f32[4]{0:T(128)}, u32[]{:S(2)}) copy-start(f32[4]{0:T(128)} %param.37) | copy-start | bytes 52
  537.1 52.6 %copy-start.4 = (f32[3,128,256]{2,1,0:T(8,128)S(1)}, f32[3,128,256]{2,1,0:T(8,128)}, u32[]{:S(2)}) copy-start(f32[3,128,256]{2,1,0:T(8,128)} %refs_11_.1) | copy-start | bytes 1179652
  537.1 52.6 %copy-start.5 = (f32[3,128,256]{2,1,0:T(8,128)S(1)}, f32[3,128,256]{2,1,0:T(8,128)}, u32[]{:S(2)}) copy-start(f32[3,128,256]{2,1,0:T(8,128)} %refs_12_.1) | copy-start | bytes 1179652
  537.1 52.6 %copy-start.6 = (f32[2,256,128]{2,1,0:T(8,128)S(1)}, f32[2,256,128]{2,1,0:T(8,128)}, u32[]{:S(2)}) copy-start(f32[2,256,128]{2,1,0:T(8,128)} %param.47) | copy-start | bytes 786436
  537.1 52.5 %copy-start.8 = (f32[2,128,256]{2,1,0:T(8,128)S(1)}, f32[2,128,256]{2,1,0:T(8,128)}, u32[]{:S(2)}) copy-start(f32[2,128,256]{2,1,0:T(8,128)} %refs_19_.1) | copy-start | bytes 786436
  537.1 52.5 %copy-start.9 = (f32[2,128,256]{2,1,0:T(8,128)S(1)}, f32[2,128,256]{2,1,0:T(8,128)}, u32[]{:S(2)}) copy-start(f32[2,128,256]{2,1,0:T(8,128)} %refs_20_.1) | copy-start | bytes 786436
  537.2 52.5 %copy-start.10 = (f32[256,128]{1,0:T(8,128)S(1)}, f32[256,128]{1,0:T(8,128)}, u32[]{:S(2)}) copy-start(f32[256,128]{1,0:T(8,128)} %param.48) | copy-start | bytes 393220
  537.2 52.5 %copy-start.11 = (f32[256,128]{1,0:T(8,128)S(1)}, f32[256,128]{1,0:T(8,128)}, u32[]{:S(2)}) copy-start(f32[256,128]{1,0:T(8,128)} %param.49) | copy-start | bytes 393220
  537.2 52.5 %copy-start.12 = (f32[256,128]{1,0:T(8,128)S(1)}, f32[256,128]{1,0:T(8,128)}, u32[]{:S(2)}) copy-start(f32[256,128]{1,0:T(8,128)} %param.57) | copy-start | bytes 393220
  537.2 52.5 %copy-start.13 = (f32[256,128]{1,0:T(8,128)S(1)}, f32[256,128]{1,0:T(8,128)}, u32[]{:S(2)}) copy-start(f32[256,128]{1,0:T(8,128)} %param.58) | copy-start | bytes 393220
  537.2 52.5 %copy-start.21 = (f32[31,256]{1,0:T(8,128)S(1)}, f32[31,256]{1,0:T(8,128)}, u32[]{:S(2)}) copy-start(f32[31,256]{1,0:T(8,128)} %param.54) | copy-start | bytes 95236
  537.2 52.5 %copy-start.22 = (f32[31,256]{1,0:T(8,128)S(1)}, f32[31,256]{1,0:T(8,128)}, u32[]{:S(2)}) copy-start(f32[31,256]{1,0:T(8,128)} %param.55) | copy-start | bytes 95236
  662.1 18.0 %copy-start.20 = (bf16[2,256,1024]{2,1,0:T(8,128)(2,1)S(1)}, bf16[2,256,1024]{2,1,0:T(8,128)(2,1)}, u32[]{:S(2)}) copy-start(bf16[2,256,1024]{2,1,0:T(8,128)(2,1)} %copy-done.19) | copy-start | bytes 3145732
  (39 other events, 89.7 us)
